TPU v7x, 512 devices: a whole 4x4x16 slice. The times are simulated.
512 devices in a mesh: rows: 128 (over y, x_lo, z), band: 4 (over x_hi, core).
Axes of the slice: x: 4 (x_hi: 2, x_lo: 2; x = x_hi * 2 + x_lo), y: 4, z: 16, core: 2. Of those that a mesh axis runs over, the one named last changes fastest.
Arguments:
- embedding: bfloat16 [16384, 512], P('rows'), may hold values from -6 to 6
- w_left: bfloat16 [512, 32], replicated, may hold values from -0.25 to 0.25
- w_right: bfloat16 [512, 32], replicated, may hold values from -0.25 to 0.25
- w_in: bfloat16 [32, 128], replicated, may hold values from -1 to 1
- w_out: bfloat16 [128, 32], replicated, may hold values from -0.5 to 0.5
- w_head: float32 [32], replicated, may hold values from -1 to 1
- dist_bias: float32 [32, 4], replicated, may hold values from -3 to 3
- offsets: int32 [128, 4], P('rows', 'band'), may hold values from 0 to 3, each once within a row
- valid_bins: int32 [16384], P('rows'), may hold values 0 or 1
- target: bfloat16 [128, 4, 128, 128], P('rows', 'band'), may hold values from -6 to 6
Outputs:
- predicted: bfloat16 [128, 4, 128, 128], P('rows', 'band')
- grad_embedding: bfloat16 [16384, 512], P('rows', 'band')
- grad_left: float32 [512, 32], replicated
- grad_right: float32 [512, 32], replicated
- grad_in: float32 [32, 128], replicated
- grad_out: float32 [128, 32], replicated
- grad_head: float32 [32], replicated
- grad_bias: float32 [32, 4], replicated
Inputs may be any that keep to these rules, and one draw needn't show every extreme that they name: `offsets`: each row tile's 4 entries are the numbers 0 to 3 in some order.
All inputs are finite; a program needn't handle non-finite values. No bound on the sum of `valid_bins` on one device may be relied on, other than what follows from the above.
Results may differ from a plain program's by a relative error of at most 0.0058.
Values may be sent and summed in bfloat16 or wider, within the bound.
A program may use at most 64 MiB of HBM per device.

v0:
```python
import functools

import jax
import jax.numpy as jnp
from jax import lax
from jax.sharding import Mesh
from jax.sharding import PartitionSpec as P

TILE = 128
NOFF = 4
ROWS = ("rows_0", "rows_1", "rows_2")
ROWS_BAND = ("rows_0", "rows_1", "rows_2", "band")


def from_behind(value, axis, steps):
    count = lax.axis_size(axis)
    leading, last = (max(0, -steps), min(count, count - steps))
    return lax.ppermute(value, axis, [(source, source + steps) for source in range(leading, last)])


def copy_for_each(array, axis):
    devices = lax.axis_size(axis)
    return lax.all_to_all(
        jnp.broadcast_to(array[None], (devices, *array.shape)), axis, 0, 0, tiled=True
    )


def taken_together(array, axis):
    everything = copy_for_each(array, axis)
    return jnp.sum(everything, axis=0)


def packed_total(arrays, axis):
    ravelled, at, gathered = (jnp.concatenate([a.reshape(-1) for a in arrays]), 0, [])
    subtotal = taken_together(ravelled, axis)
    for a in arrays:
        gathered.append(subtotal[at : at + a.size].reshape(a.shape))
        at += a.size
    return tuple(gathered)


def over_axes(array, axes):
    return functools.reduce(lax.psum, axes, array)


def side_by_side(arrays, axis, dim, along):
    ends, at = ([], 0)
    for a in arrays[:-1]:
        at += a.shape[along]
        ends.append(at)
    both = jnp.concatenate(arrays, axis=along)
    return tuple(jnp.split(lax.all_gather(both, axis, axis=dim, tiled=True), ends, axis=along))


def gelu_pair(pre_act):
    return jax.nn.gelu(pre_act, approximate=True)


def block_terms(row_proj, col_proj, bias_col, row_flags, col_flags, goal_rows, w_in, w_out, w_head):
    channels = row_proj.shape[0]
    row_count = row_proj.shape[1]
    col_count = col_proj.shape[1]
    summed = (
        row_proj.astype(jnp.float32)[:, :, None]
        + col_proj.astype(jnp.float32)[:, None, :]
        + bias_col[:, None, None]
    )
    summed = summed.reshape(channels, row_count * col_count)
    pair_in = summed.astype(jnp.bfloat16)
    pre_act = lax.dot_general(
        w_in, pair_in, (((0,), (0,)), ((), ())), preferred_element_type=jnp.float32
    )
    activation = gelu_pair(pre_act).astype(jnp.bfloat16)
    update = summed + lax.dot_general(
        w_out, activation, (((0,), (0,)), ((), ())), preferred_element_type=jnp.float32
    )
    logits = jnp.dot(w_head, update, precision=lax.Precision.HIGHEST)
    weight_mask = (row_flags[:, None] * col_flags[None, :]).reshape(-1)
    residual = weight_mask * (logits - goal_rows.astype(jnp.float32).reshape(-1)) / (NOFF * TILE)
    grad_update = w_head[:, None] * residual[None, :]
    grad_low = grad_update.astype(jnp.bfloat16)
    head_term = jnp.dot(update, residual, precision=lax.Precision.HIGHEST)
    out_term = lax.dot_general(
        activation, grad_low, (((1,), (1,)), ((), ())), preferred_element_type=jnp.float32
    )
    grad_act = lax.dot_general(
        w_out, grad_low, (((1,), (0,)), ((), ())), preferred_element_type=jnp.float32
    )
    _, backward = jax.vjp(gelu_pair, pre_act)
    grad_pre = backward(grad_act)[0].astype(jnp.bfloat16)
    in_term = lax.dot_general(
        pair_in, grad_pre, (((1,), (1,)), ((), ())), preferred_element_type=jnp.float32
    )
    grad_pair = grad_update + lax.dot_general(
        w_in, grad_pre, (((1,), (0,)), ((), ())), preferred_element_type=jnp.float32
    )
    grad_cube = grad_pair.reshape(channels, row_count, col_count)
    return (
        logits.reshape(row_count, col_count),
        head_term,
        out_term,
        in_term,
        jnp.sum(grad_pair, axis=1),
        jnp.sum(grad_cube, axis=2),
        jnp.sum(grad_cube, axis=1),
    )


def tile_terms(row_proj, col_proj, bias_col, row_flags, col_flags, goal_tile, w_in, w_out, w_head):
    half_rows = row_proj.shape[1] // 2
    first = block_terms(
        row_proj[:, :half_rows],
        col_proj,
        bias_col,
        row_flags[:half_rows],
        col_flags,
        goal_tile[:half_rows],
        w_in,
        w_out,
        w_head,
    )
    second = block_terms(
        row_proj[:, half_rows:],
        col_proj,
        bias_col,
        row_flags[half_rows:],
        col_flags,
        goal_tile[half_rows:],
        w_in,
        w_out,
        w_head,
    )
    return (
        jnp.concatenate([first[0], second[0]], axis=0),
        first[1] + second[1],
        first[2] + second[2],
        first[3] + second[3],
        first[4] + second[4],
        jnp.concatenate([first[5], second[5]], axis=1),
        first[6] + second[6],
    )


def project(embedding, weight):
    return lax.dot_general(
        weight, embedding, (((0,), (1,)), ((), ())), preferred_element_type=jnp.float32
    ).astype(jnp.bfloat16)


def fetch_ahead(right_proj, flags_low, step_count):
    return from_behind((right_proj, flags_low), ROWS, -step_count)


def return_behind(col_piece, step_count):
    return from_behind(col_piece, ROWS, step_count)


def on_device(
    embedding, w_left, w_right, w_in, w_out, w_head, dist_bias, offsets, valid_bins, target
):
    bin_count = embedding.shape[0]
    tile_count = bin_count // TILE
    slot_count = offsets.shape[1]
    reach_count = (NOFF + tile_count - 2) // tile_count
    channels = w_left.shape[1]
    hidden = w_in.shape[1]
    left_proj = project(embedding, w_left)
    right_proj = project(embedding, w_right)
    flags_low = valid_bins.astype(jnp.bfloat16)
    proj_parts = [right_proj]
    flag_parts = [flags_low]
    for step_count in range(1, reach_count + 1):
        moved_proj, moved_flags = fetch_ahead(right_proj, flags_low, step_count)
        proj_parts.append(moved_proj)
        flag_parts.append(moved_flags)
    right_ext = jnp.concatenate(proj_parts, axis=1)
    flags_ext = jnp.concatenate(flag_parts, axis=0).astype(jnp.float32)
    extended = bin_count * (reach_count + 1)
    initial = (
        jnp.zeros((channels, bin_count), jnp.float32),
        jnp.zeros((channels, extended), jnp.float32),
        jnp.zeros((channels, hidden), jnp.float32),
        jnp.zeros((hidden, channels), jnp.float32),
        jnp.zeros((channels,), jnp.float32),
        jnp.zeros((channels, NOFF), jnp.float32),
    )

    def advance(totals, item_index):
        tile_row = item_index // slot_count
        slot_index = item_index % slot_count
        offset = offsets[tile_row, slot_index]
        one_hot = (jnp.arange(NOFF, dtype=jnp.int32) == offset).astype(jnp.float32)
        bias_col = jnp.sum(dist_bias * one_hot[None, :], axis=1)
        row_start = tile_row * TILE
        col_start = (tile_row + offset) * TILE
        col_proj = lax.dynamic_slice_in_dim(right_ext, col_start, TILE, 1)
        row_flags = lax.dynamic_slice_in_dim(flags_ext, row_start, TILE, 0)
        col_flags = lax.dynamic_slice_in_dim(flags_ext, col_start, TILE, 0)
        goal_tile = target[tile_row, slot_index]
        logits, head_term, out_term, in_term, bias_sum, row_sums, col_sums = tile_terms(
            left_proj, col_proj, bias_col, row_flags, col_flags, goal_tile, w_in, w_out, w_head
        )
        row_acc, col_acc, in_acc, out_acc, head_acc, bias_acc = totals
        row_acc = row_acc + row_sums
        col_acc = lax.dynamic_update_slice_in_dim(
            col_acc, lax.dynamic_slice_in_dim(col_acc, col_start, TILE, 1) + col_sums, col_start, 1
        )
        bias_acc = bias_acc + bias_sum[:, None] * one_hot[None, :]
        return (
            (
                row_acc,
                col_acc,
                in_acc + in_term,
                out_acc + out_term,
                head_acc + head_term,
                bias_acc,
            ),
            logits,
        )

    totals, logits = lax.scan(
        advance, initial, jnp.arange(tile_count * slot_count, dtype=jnp.int32)
    )
    row_acc, col_acc, in_part, out_part, head_part, bias_part = totals
    predicted = logits.reshape(tile_count, slot_count, TILE, TILE).astype(jnp.bfloat16)
    col_own = col_acc[:, :bin_count]
    for step_count in range(1, reach_count + 1):
        col_piece = col_acc[:, step_count * bin_count : (step_count + 1) * bin_count]
        col_own = col_own + return_behind(col_piece, step_count)
    row_total, col_total = packed_total((row_acc, col_own), "band")
    row_grad = row_total.astype(jnp.bfloat16)
    col_grad = col_total.astype(jnp.bfloat16)
    grad_in, grad_out, grad_head, grad_bias = lax.psum(
        (in_part, out_part, head_part, bias_part), ROWS_BAND
    )
    share = embedding.shape[1] // lax.axis_size("band")
    share_start = lax.axis_index("band") * share
    left_share = lax.dynamic_slice_in_dim(w_left, share_start, share, 0)
    right_share = lax.dynamic_slice_in_dim(w_right, share_start, share, 0)
    grad_embedding = (
        lax.dot_general(
            row_grad, left_share, (((0,), (1,)), ((), ())), preferred_element_type=jnp.float32
        )
        + lax.dot_general(
            col_grad, right_share, (((0,), (1,)), ((), ())), preferred_element_type=jnp.float32
        )
    ).astype(jnp.bfloat16)
    embed_share = lax.dynamic_slice_in_dim(embedding, share_start, share, 1)
    left_part = lax.dot_general(
        embed_share, row_grad, (((0,), (1,)), ((), ())), preferred_element_type=jnp.float32
    )
    right_part = lax.dot_general(
        embed_share, col_grad, (((0,), (1,)), ((), ())), preferred_element_type=jnp.float32
    )
    left_sum, right_sum = (over_axes(left_part, ROWS), over_axes(right_part, ROWS))
    grad_left, grad_right = side_by_side((left_sum, right_sum), "band", 0, 1)
    return (
        predicted,
        grad_embedding,
        grad_left,
        grad_right,
        grad_in,
        grad_out,
        grad_head,
        grad_bias,
    )


def solution(mesh):
    torus = Mesh(
        mesh.devices.reshape(4, 2, 16, mesh.shape["band"]), ("rows_0", "rows_1", "rows_2", "band")
    )
    placed = (
        P(ROWS, None),
        P(),
        P(),
        P(),
        P(),
        P(),
        P(),
        P(ROWS, "band"),
        P(ROWS),
        P(ROWS, "band", None, None),
    )
    return jax.shard_map(
        on_device,
        mesh=torus,
        in_specs=placed,
        out_specs=(P(ROWS, "band", None, None), P(ROWS, "band"), P(), P(), P(), P(), P(), P()),
        check_vma=False,
    )
```

profile of v0, /device:TPU:1, one launch (start us, length us, event | category | flops | bytes accessed | tf_op | source)
XLA Modules:
  0.0 276.8 jit_solution(2676862389317497101)
XLA Ops:
  0.6 0.0 copy-start
  0.6 0.9 copy-done
  1.5 0.9 convolution_convert_fusion
  2.4 1.3 collective-permute-start
  3.7 1.3 collective-permute-start.1
  5.0 0.7 convert_element_type.111
  5.7 1.3 collective-permute-start.3
  7.0 1.3 collective-permute-start.4
  8.3 1.3 collective-permute-start.5
  10.2 0.9 convolution_convert_fusion.1
  11.1 0.1 slice_convert_fusion.1
  11.2 0.8 multiply_reduce_fusion
  12.0 1.3 collective-permute-start.2
  13.3 2.2 collective-permute-done.4
  15.5 3.3 %collective-permute-done.5 = bf16[128]{0:T(256)(128)(2,1)S(1)} collective-permute-done((bf16[128]{0:T(256)(128)(2,1)S(1)}, bf16[128]{0:T(256)(128)(2,1)S(1)}, u32[]{:S(2)}, u32[]{:S(2)}) %collective-permute-start.5) | collective-permute-done | bytes 288 | tf_op jit(solution)/shard_map/ppermute | solution.py:18
  18.8 0.1 fusion.64
  18.9 0.1 dynamic_slice.29
  19.0 4.3 %collective-permute-done.2 = bf16[32,128]{1,0:T(8,128)(2,1)S(1)} collective-permute-done((bf16[32,128]{1,0:T(8,128)(2,1)S(1)}, bf16[32,128]{1,0:T(8,128)(2,1)S(1)}, u32[]{:S(2)}, u32[]{:S(2)}) %collective-permute-start.2) | collective-permute-done | bytes 8224 | tf_op jit(solution)/shard_map/ppermute | solution.py:18
  23.3 0.6 broadcast_add_fusion.1
  23.9 0.0 copy-start.2
  23.9 2.7 multiply_convert_fusion.1
  26.7 0.0 copy-start.1
  26.7 2.0 multiply_convert_fusion
  28.7 0.0 copy-start.4
  28.7 1.0 fusion.3
  29.7 1.0 fusion.2
  30.7 0.7 fusion.55
  31.3 0.7 fusion.53
  32.0 0.1 fusion.32
  32.1 0.5 fusion.22
  32.6 3.7 %fusion.10 = bf16[128,8192]{0,1:T(8,128)(2,1)S(1)} fusion(f32[128,8192]{0,1:T(8,128)S(1)} %get-tuple-element.87, bf16[128,32]{0,1:T(8,128)(2,1)S(1)} %copy-done.1, f32[8192]{0:T(1024)S(1)} %get-tuple-element.75, f32[32]{0:T(128)S(1)} %copy-done.4), kind=kOutput, calls=%fused_computation.22 | convolution fusion | flops 88604672 | bytes 6332544 | tf_op jit(solution)/shard_map/while/body/eval_jaxpr/dot_general | solution.py:86
  36.3 0.9 fusion.65
  37.2 0.8 fusion.59
  38.0 3.5 %fusion.17 = bf16[128,8192]{0,1:T(8,128)(2,1)S(1)} fusion(f32[128,8192]{0,1:T(8,128)S(1)} %get-tuple-element.85, bf16[128,32]{0,1:T(8,128)(2,1)S(1)} %copy-done.1, f32[8192]{0:T(1024)S(1)} %get-tuple-element.74, f32[32]{0:T(128)S(1)} %copy-done.4), kind=kOutput, calls=%fused_computation.29 | convolution fusion | flops 88604672 | bytes 6332544 | tf_op jit(solution)/shard_map/while/body/eval_jaxpr/dot_general | solution.py:86
  41.5 0.9 fusion.66
  42.4 0.1 broadcast_multiply_fusion
  42.5 0.9 convolution_bitcast_fusion.8
  43.4 0.5 convolution_add_fusion.1
  43.9 0.8 convolution_add_fusion.2
  44.8 0.2 copy.22
  44.9 0.2 copy.23
  45.1 0.2 bitcast_reduce_fusion
  45.3 0.3 reduce_sum.80
  45.6 0.3 reduce_sum.81
  46.0 4.8 %collective-permute-start.6 = (f32[32,128]{1,0:T(8,128)S(1)}, f32[32,128]{1,0:T(8,128)S(1)}, u32[]{:S(2)}, u32[]{:S(2)}) collective-permute-start(f32[32,128]{1,0:T(8,128)S(1)} %get-tuple-element.71), channel_id=1, source_target_pairs={{0,4},{4,8},{8,12},{12,16},{16,20},{20,24},{24,28},{28,32},{32,36}... | collective-permute-start | bytes 49160 | tf_op jit(solution)/shard_map/ppermute | solution.py:18
  50.8 4.9 %collective-permute-start.7 = (f32[32,128]{1,0:T(8,128)S(1)}, f32[32,128]{1,0:T(8,128)S(1)}, u32[]{:S(2)}, u32[]{:S(2)}) collective-permute-start(f32[32,128]{1,0:T(8,128)S(1)} %get-tuple-element.73), channel_id=1, source_target_pairs={{0,8},{4,12},{8,16},{12,20},{16,24},{20,28},{24,32},{28,36},{32,40... | collective-permute-start | bytes 49160 | tf_op jit(solution)/shard_map/ppermute | solution.py:18
  55.7 7.3 %collective-permute-start.8 = (f32[32,128]{1,0:T(8,128)S(1)}, f32[32,128]{1,0:T(8,128)S(1)}, u32[]{:S(2)}, u32[]{:S(2)}) collective-permute-start(f32[32,128]{1,0:T(8,128)S(1)} %get-tuple-element.72), channel_id=1, source_target_pairs={{0,12},{4,16},{8,20},{12,24},{16,28},{20,32},{24,36},{28,40},{32,4... | collective-permute-start | bytes 49160 | tf_op jit(solution)/shard_map/ppermute | solution.py:18
  63.0 1.0 fusion.19
  63.9 0.1 maximum_bitcast_fusion
  64.0 114.1 %all-reduce = (f32[32,128]{1,0:T(8,128)}, f32[128,32]{0,1:T(8,128)}, f32[32]{0:T(128)}, f32[32,4]{0,1:T(4,128)}) all-reduce(f32[32,128]{1,0:T(8,128)S(1)} %convolution_add_fusion.2, f32[128,32]{0,1:T(8,128)S(1)} %convolution_add_fusion.1, ...), channel_id=1, replica_groups=mesh['rows_0'=4,'rows_1'=2,'rows_2'=16,'band'=4] {'rows_0','rows_1','row..., use_global_device_ids=true, to_apply=%region_12.13 | all-reduce | flops 8352 | bytes 66816 | tf_op jit(solution)/shard_map/psum | solution.py:233
  178.2 0.7 broadcast_in_dim.19
  178.9 4.1 %all-to-all-start = ((f32[4,1,8192]{2,1,0:T(1,128)}), f32[4,1,8192]{2,1,0:T(1,128)S(1)}, u32[]{:S(2)}, u32[]{:S(2)}) async-start(f32[4,1,8192]{2,1,0:T(1,128)} %broadcast_in_dim.19), calls=%async_computation | async-start | bytes 262144 | tf_op jit(solution)/shard_map/all_to_all | solution.py:23
  183.0 0.6 pad_maximum_fusion
  183.6 4.5 %all-to-all-done = f32[4,1,8192]{2,1,0:T(1,128)S(1)} async-done(((f32[4,1,8192]{2,1,0:T(1,128)}), f32[4,1,8192]{2,1,0:T(1,128)S(1)}, u32[]{:S(2)}, u32[]{:S(2)}) %all-to-all-start) | async-done | bytes 131104 | tf_op jit(solution)/shard_map/all_to_all | solution.py:23
  188.1 0.1 reduce_sum.84
  188.3 0.1 fusion.35
  188.4 0.1 fusion.37
  188.5 0.9 fusion.47
  189.4 12.2 %all-reduce.2 = (f32[128,32]{0,1:T(8,128)S(1)}, f32[128,32]{0,1:T(8,128)S(1)}) all-reduce(f32[128,32]{0,1:T(8,128)S(1)} %fusion.37, f32[128,32]{0,1:T(8,128)S(1)} %fusion.35), channel_id=1, replica_groups=mesh['rows_0'=4,'rows_1'=2,'rows_2'=16,'band'=4] {'rows_0'}, use_global_device_ids=true, to_apply=%region_9.10 | all-reduce | flops 8192 | bytes 65536 | tf_op jit(solution)/shard_map/psum | solution.py:43
  201.6 6.1 %all-reduce.3 = (f32[128,32]{0,1:T(8,128)S(1)}, f32[128,32]{0,1:T(8,128)S(1)}) all-reduce(f32[128,32]{0,1:T(8,128)S(1)} %get-tuple-element.48, f32[128,32]{0,1:T(8,128)S(1)} %get-tuple-element.49), channel_id=1, replica_groups=mesh['rows_0'=4,'rows_1'=2,'rows_2'=16,'band'=4] {'rows_1'}, use_global_device_ids=true, to_apply=%region_10.11 | all-reduce | flops 8192 | bytes 65536 | tf_op jit(solution)/shard_map/psum | solution.py:43
  207.7 39.7 %all-reduce.1 = (f32[128,32]{0,1:T(8,128)S(1)}, f32[128,32]{0,1:T(8,128)S(1)}) all-reduce(f32[128,32]{0,1:T(8,128)S(1)} %get-tuple-element.50, f32[128,32]{0,1:T(8,128)S(1)} %get-tuple-element.68), channel_id=1, replica_groups=mesh['rows_0'=4,'rows_1'=2,'rows_2'=16,'band'=4] {'rows_2'}, use_global_device_ids=true, to_apply=%region_11.12 | all-reduce | flops 8192 | bytes 65536 | tf_op jit(solution)/shard_map/psum | solution.py:43
  247.4 27.2 %all_gather.3 = f32[512,64]{0,1:T(8,128)S(1)} all-gather(f32[128,64]{0,1:T(8,128)S(1)} %pad_maximum_fusion.2), channel_id=1, replica_groups=mesh['rows_0'=4,'rows_1'=2,'rows_2'=16,'band'=4] {'band'}, dimensions={0}, use_global_device_ids=true | all-gather | bytes 163840 | tf_op jit(solution)/shard_map/all_gather | solution.py:52
  274.6 0.7 fusion.62
  275.3 1.5 fusion.18
  (21 shorter events, 0.1 us)
Async XLA Ops:
  0.6 0.9 copy-start
  2.4 16.5 %collective-permute-start = (bf16[32,128]{1,0:T(8,128)(2,1)S(1)}, bf16[32,128]{1,0:T(8,128)(2,1)S(1)}, u32[]{:S(2)}, u32[]{:S(2)}) collective-permute-start(bf16[32,128]{1,0:T(8,128)(2,1)S(1)} %convolution_convert_fusion), channel_id=1, source_target_pairs={{4,0},{8,4},{12,8},{16,12},{20,16},{24,20},{28,24},{32,28},{36,32}... | collective-permute-start | bytes 24584 | tf_op jit(solution)/shard_map/ppermute | solution.py:18
  3.7 15.2 %collective-permute-start.1 = (bf16[32,128]{1,0:T(8,128)(2,1)S(1)}, bf16[32,128]{1,0:T(8,128)(2,1)S(1)}, u32[]{:S(2)}, u32[]{:S(2)}) collective-permute-start(bf16[32,128]{1,0:T(8,128)(2,1)S(1)} %convolution_convert_fusion), channel_id=1, source_target_pairs={{8,0},{12,4},{16,8},{20,12},{24,16},{28,20},{32,24},{36,28},{40,32... | collective-permute-start | bytes 24584 | tf_op jit(solution)/shard_map/ppermute | solution.py:18
  5.7 6.3 %collective-permute-start.3 = (bf16[128]{0:T(256)(128)(2,1)S(1)}, bf16[128]{0:T(256)(128)(2,1)S(1)}, u32[]{:S(2)}, u32[]{:S(2)}) collective-permute-start(bf16[128]{0:T(256)(128)(2,1)S(1)} %convert_element_type.111), channel_id=1, source_target_pairs={{4,0},{8,4},{12,8},{16,12},{20,16},{24,20},{28,24},{32,28},{36,32}... | collective-permute-start | bytes 776 | tf_op jit(solution)/shard_map/ppermute | solution.py:18
  7.0 8.5 %collective-permute-start.4 = (bf16[128]{0:T(256)(128)(2,1)S(1)}, bf16[128]{0:T(256)(128)(2,1)S(1)}, u32[]{:S(2)}, u32[]{:S(2)}) collective-permute-start(bf16[128]{0:T(256)(128)(2,1)S(1)} %convert_element_type.111), channel_id=1, source_target_pairs={{8,0},{12,4},{16,8},{20,12},{24,16},{28,20},{32,24},{36,28},{40,32... | collective-permute-start | bytes 776 | tf_op jit(solution)/shard_map/ppermute | solution.py:18
  8.3 10.5 %collective-permute-start.5 = (bf16[128]{0:T(256)(128)(2,1)S(1)}, bf16[128]{0:T(256)(128)(2,1)S(1)}, u32[]{:S(2)}, u32[]{:S(2)}) collective-permute-start(bf16[128]{0:T(256)(128)(2,1)S(1)} %convert_element_type.111), channel_id=1, source_target_pairs={{12,0},{16,4},{20,8},{24,12},{28,16},{32,20},{36,24},{40,28},{44,3... | collective-permute-start | bytes 776 | tf_op jit(solution)/shard_map/ppermute | solution.py:18
  12.0 11.3 %collective-permute-start.2 = (bf16[32,128]{1,0:T(8,128)(2,1)S(1)}, bf16[32,128]{1,0:T(8,128)(2,1)S(1)}, u32[]{:S(2)}, u32[]{:S(2)}) collective-permute-start(bf16[32,128]{1,0:T(8,128)(2,1)S(1)} %convolution_convert_fusion), channel_id=1, source_target_pairs={{12,0},{16,4},{20,8},{24,12},{28,16},{32,20},{36,24},{40,28},{44,3... | collective-permute-start | bytes 24584 | tf_op jit(solution)/shard_map/ppermute | solution.py:18
  23.9 2.8 %copy-start.2 = (bf16[32,128]{1,0:T(8,128)(2,1)S(1)}, bf16[32,128]{1,0:T(8,128)(2,1)}, u32[]{:S(2)}) copy-start(bf16[32,128]{1,0:T(8,128)(2,1)} %param.13) | copy-start | bytes 24580
  26.7 2.0 copy-start.1
  28.7 2.0 copy-start.4
  29.7 2.3 copy-start.3
  46.0 132.1 %collective-permute-start.6 = (f32[32,128]{1,0:T(8,128)S(1)}, f32[32,128]{1,0:T(8,128)S(1)}, u32[]{:S(2)}, u32[]{:S(2)}) collective-permute-start(f32[32,128]{1,0:T(8,128)S(1)} %get-tuple-element.71), channel_id=1, source_target_pairs={{0,4},{4,8},{8,12},{12,16},{16,20},{20,24},{24,28},{28,32},{32,36}... | collective-permute-start | bytes 49160 | tf_op jit(solution)/shard_map/ppermute | solution.py:18
  50.8 127.4 %collective-permute-start.7 = (f32[32,128]{1,0:T(8,128)S(1)}, f32[32,128]{1,0:T(8,128)S(1)}, u32[]{:S(2)}, u32[]{:S(2)}) collective-permute-start(f32[32,128]{1,0:T(8,128)S(1)} %get-tuple-element.73), channel_id=1, source_target_pairs={{0,8},{4,12},{8,16},{12,20},{16,24},{20,28},{24,32},{28,36},{32,40... | collective-permute-start | bytes 49160 | tf_op jit(solution)/shard_map/ppermute | solution.py:18
  55.7 122.5 %collective-permute-start.8 = (f32[32,128]{1,0:T(8,128)S(1)}, f32[32,128]{1,0:T(8,128)S(1)}, u32[]{:S(2)}, u32[]{:S(2)}) collective-permute-start(f32[32,128]{1,0:T(8,128)S(1)} %get-tuple-element.72), channel_id=1, source_target_pairs={{0,12},{4,16},{8,20},{12,24},{16,28},{20,32},{24,36},{28,40},{32,4... | collective-permute-start | bytes 49160 | tf_op jit(solution)/shard_map/ppermute | solution.py:18
  178.9 9.2 %all-to-all-start = ((f32[4,1,8192]{2,1,0:T(1,128)}), f32[4,1,8192]{2,1,0:T(1,128)S(1)}, u32[]{:S(2)}, u32[]{:S(2)}) async-start(f32[4,1,8192]{2,1,0:T(1,128)} %broadcast_in_dim.19), calls=%async_computation | async-start | bytes 262144 | tf_op jit(solution)/shard_map/all_to_all | solution.py:23
where the time goes:
time: 278 us; the launch traced here: 277 us
  blocking collectives  199 us (72%)
  starting transfers between devices  28.8 us (10%)
  matrix products  25.9 us (9%)
  waiting for transfers between devices  14.3 us (5%)
  other arithmetic  4.02 us (1%)
  local copies, waits for them, and re-layouts  2.83 us (1%)
    psum x1, blocking collectives, on_device(): lax.psum((in_part, out_part, head_part, bias_part), ROWS_BAND)  114 us
    psum x3, blocking collectives, over_axes(): return functools.reduce(lax.psum, axes, array)  58 us
    all_gather x1, blocking collectives, side_by_side(): lax.all_gather(both, axis, axis=dim, tiled=True)  27.2 us
    ppermute x9, starting transfers between devices, from_behind(): lax.ppermute(value, axis, [(source, source + steps) for source in range(l...  24.7 us
    ppermute x9, waiting for transfers between devices, from_behind(): lax.ppermute(value, axis, [(source, source + steps) for source in range(l...  9.81 us
    dot_general x2, matrix products, block_terms(): lax.dot_general(w_out, grad_low, (((1,), (0,)), ((), ())), preferred_elem...  7.13 us
  transfers between devices with their start and end apart: 10, of which 4 were waited for; matrix products, arithmetic and copies ran while one was open for 2% of the time, Pallas kernels for 0%

commit v1 on v0

v1 whole, which is shorter than its diff:
```python
import functools

import jax
import jax.numpy as jnp
from jax import lax
from jax.experimental import pallas as pl
from jax.experimental.pallas import tpu as pltpu
from jax.sharding import PartitionSpec as P

TILE = 128
NOFF = 4
CH = 32
HID = 128
ROWS = 128
RING = 16
GROUPS = 8
BAND = 4
MESH = pl.DeviceIdType.MESH
F32 = jnp.float32
BF16 = jnp.bfloat16

C0 = 0.7978845608028654
C1 = C0 * 0.044715
ALPHA = C1 ** (-1.0 / 3.0)
BETA = C0 * ALPHA


def hdot(a, b, ca, cb):
    return lax.dot_general(
        a, b, (((ca,), (cb,)), ((), ())), precision=lax.Precision.HIGHEST, preferred_element_type=F32
    )


def bdot(a, b, ca, cb):
    return lax.dot_general(a, b, (((ca,), (cb,)), ((), ())), preferred_element_type=F32)


def kernel(
    off_ref, emb, wl, wr, win, wout, whead, dbias, vbins, tgt,
    pred, gemb, gl, gr, gin, gout, gex,
    abc, act, slope, b_s, v_s, gr_s, gc_s, ar_s,
    pay, pay_in, e_in,
    x_out, x_in, s_out, s_in, small,
    rs_out, rs_in, zbuf, fin, c_out, c_in,
    pay_ss, pay_rs, e_ss, e_rs, x_ss, x_rs, s_ss, s_rs, g_ss, g_rs, z_ss, z_rs, f_ss, f_rs, c_ss, c_rs,
):
    r = lax.axis_index("rows")
    b = lax.axis_index("band")
    z = lax.rem(r, RING)
    base = r - z
    g = lax.div(r, RING)

    def row_at(d):
        return lax.rem(r + (d + ROWS), ROWS)

    def ring_at(d):
        return base + lax.rem(z + d, RING)

    def group_at(d):
        return lax.rem(r + RING * d, ROWS)

    def band_at(d):
        return lax.rem(b + d, BAND)

    def remote(src, dst, ss, rs, dev):
        return pltpu.make_async_remote_copy(
            src_ref=src, dst_ref=dst, send_sem=ss, recv_sem=rs, device_id=dev, device_id_type=MESH
        )

    barrier = pltpu.get_barrier_semaphore()
    partners = [(row_at(d), b) for d in (-3, -2, -1, 1, 2, 3)]
    partners += [(ring_at(d), b) for d in range(1, RING)]
    partners += [(group_at(d), band_at(e)) for d in range(GROUPS) for e in range(BAND) if d or e]
    for dev in partners:
        pl.semaphore_signal(barrier, inc=1, device_id=dev, device_id_type=MESH)

    lt = bdot(emb[...], wl[...], 1, 0).astype(BF16)
    rt = bdot(emb[...], wr[...], 1, 0).astype(BF16)
    ltf, rtf = lt.astype(F32), rt.astype(F32)
    lr = jnp.transpose(jnp.concatenate([ltf, rtf], axis=1))
    left, right = lr[:CH], lr[CH:]
    flags = vbins[...].astype(F32)
    pay[0:CH] = right.astype(BF16)
    pay[CH:CH + 16] = jnp.broadcast_to(flags, (16, TILE)).astype(BF16)

    pl.semaphore_wait(barrier, len(partners))
    pay_c = [
        remote(pay, pay_in.at[d - 1], pay_ss.at[d - 1], pay_rs.at[d - 1], (row_at(-d), b)) for d in (3, 2, 1)
    ]
    for c in pay_c:
        c.start()

    share = pl.ds(pl.multiple_of(b * TILE, TILE), TILE)
    wh = whead[...]
    wcol = jnp.sum(
        jnp.where(
            lax.broadcasted_iota(jnp.int32, (CH, CH), 0) == lax.broadcasted_iota(jnp.int32, (CH, CH), 1), wh, 0.0
        ),
        axis=1, keepdims=True,
    )
    v_s[...] = jnp.broadcast_to(
        jnp.sum(wout[...].astype(F32) * wh, axis=1, keepdims=True), (HID, TILE)
    )
    row_logit = jnp.sum(ltf * wh, axis=1, keepdims=True)
    win_f = win[...].astype(F32)
    win_t = jnp.transpose(win_f)
    at = bdot(lt, win[...], 1, 0) * (1.0 / ALPHA)

    def spread(i, rolled):
        for j in range(8):
            abc[8 * i + j] = jnp.broadcast_to(rolled[:, j:j + 1], (TILE, TILE))
        return pltpu.roll(rolled, TILE - 8, 1)

    lax.fori_loop(0, HID // 8, spread, at)

    offset = off_ref[0, 0]
    hot = [jnp.where(offset == j, 1.0, 0.0).astype(F32) for j in range(NOFF)]
    bias_col = jnp.sum(
        jnp.where(lax.broadcasted_iota(jnp.int32, (CH, NOFF), 1) == offset, dbias[...], 0.0),
        axis=1, keepdims=True,
    )

    r_sel = right * hot[0]
    f_sel = flags * hot[0]
    for c in pay_c:
        c.wait_recv()
    for d in (1, 2, 3):
        keep = hot[d] * jnp.where(r + d < ROWS, 1.0, 0.0).astype(F32)
        r_sel = r_sel + pay_in[d - 1, 0:CH].astype(F32) * keep
        f_sel = f_sel + pay_in[d - 1, CH:CH + 16].astype(F32)[0:1] * keep

    e_c = [
        remote(emb.at[:, share], e_in.at[d - 1], e_ss.at[d - 1], e_rs.at[d - 1], (row_at(-d), b)) for d in (3, 2, 1)
    ]
    for c in e_c:
        c.start()

    r_b = r_sel + bias_col
    b_s[...] = hdot(win_t, r_b, 1, 0) * (1.0 / ALPHA)
    col_logit = jnp.sum(r_b * wcol, axis=0, keepdims=True)

    def first(i, total):
        for j in range(4):
            k = 4 * i + j
            y = abc[k] + b_s[pl.ds(k, 1), :]
            w = y * y + BETA
            t = jnp.tanh(y * w)
            q = 1.0 + t
            a2 = y * q
            act[k] = a2.astype(BF16)
            slope[k] = (q + (a2 * (1.0 - t)) * (3.0 * w - 2.0 * BETA)).astype(BF16)
            total = total + a2 * v_s[pl.ds(k, 1), :]
        return total

    total = lax.fori_loop(0, HID // 4, first, jnp.zeros((TILE, TILE), F32))
    logits = total * (0.5 * ALPHA) + (row_logit + col_logit)
    pred[...] = logits.astype(BF16)
    row_flags = jnp.sum(
        jnp.where(
            lax.broadcasted_iota(jnp.int32, (TILE, TILE), 0) == lax.broadcasted_iota(jnp.int32, (TILE, TILE), 1),
            flags, 0.0,
        ),
        axis=1, keepdims=True,
    )
    res = (row_flags * f_sel) * (logits - tgt[...].astype(F32)) * (1.0 / (NOFF * TILE))
    res_b = res.astype(BF16)
    ones = jnp.ones((8, TILE), BF16)

    def second(i, carry):
        for j in range(4):
            k = 4 * i + j
            h = slope[k] * res_b
            a = act[k] * res_b
            both = bdot(ones, jnp.concatenate([h, a], axis=1), 1, 0)
            gc_s[pl.ds(k, 1), :] = both[0:1, :TILE]
            ar_s[pl.ds(k, 1), :] = both[0:1, TILE:]
            gr_s[pl.ds(k, 1), :] = bdot(ones, h, 1, 1)[0:1]
        return carry

    lax.fori_loop(0, HID // 4, second, 0)

    ones_f = jnp.ones((8, TILE), F32)
    half_v = v_s[...] * 0.5
    g_both = jnp.concatenate([gr_s[...] * half_v, gc_s[...] * half_v], axis=1)
    rr = hdot(ones_f, res, 1, 1)
    rc = jnp.broadcast_to(jnp.sum(res, axis=0, keepdims=True), (8, TILE))
    r_both = jnp.concatenate([rr, rc], axis=1)
    p_both = jnp.concatenate([left, r_b], axis=1)
    sums = hdot(win_f, g_both, 1, 0) + wcol * r_both[0:1]
    sums_b = sums.astype(BF16)
    gin_part = hdot(p_both, g_both, 1, 1)
    head = hdot(r_both, p_both, 1, 1)
    bias = hdot(ones_f, sums[:, :TILE], 1, 1)
    ar = hdot(ones_f, ar_s[...], 1, 1)
    row_id = lax.broadcasted_iota(jnp.int32, (8, TILE), 0)
    small[...] = jnp.where(row_id == 5, ar, jnp.where(row_id == 6, offset.astype(F32), 0.0))
    for j in range(NOFF):
        small[j:j + 1, 0:CH] = bias[0:1] * hot[j]
    small[4:5, 0:CH] = head[0:1]
    extra = small[...]

    x_out[0:CH] = sums_b[:, :TILE]
    x_out[CH:2 * CH] = sums_b[:, TILE:]
    for e in range(BAND):
        s_out[e, 0:8] = gin_part[8 * e:8 * e + 8]
        s_out[e, 8:16] = extra
    x_c, s_c = [], []
    for e in (2, 3, 1):
        dev = (r, band_at(e))
        x_c.append(remote(x_out, x_in.at[e - 1], x_ss.at[e - 1], x_rs.at[e - 1], dev))
        s_c.append(remote(s_out.at[band_at(e)], s_in.at[e - 1], s_ss.at[e - 1], s_rs.at[e - 1], dev))
    for c, s in zip(x_c, s_c):
        c.start()
        s.start()
    for c in e_c:
        c.wait_recv()
    for c, s in zip(x_c, s_c):
        c.wait_recv()
        s.wait_recv()
    own = x_out[...].astype(F32)
    row_tot = own[:CH]
    cols = [own[CH:] * hot[j] for j in range(NOFF)]
    mine = s_out[b]
    for e in range(BAND - 1):
        got = x_in[e].astype(F32)
        its = s_in[e]
        row_tot = row_tot + got[:CH]
        its_offset = its[14:15, :]
        for j in range(NOFF):
            cols[j] = cols[j] + jnp.where(its_offset == j, got[CH:], 0.0)
        mine = mine + its
    row_b = row_tot.astype(BF16)
    cols_b = [c.astype(BF16) for c in cols]
    part_l = bdot(row_b, emb[:, share], 1, 0)
    part_r = bdot(cols_b[0], emb[:, share], 1, 0)
    for d in (1, 2, 3):
        part_r = part_r + bdot(cols_b[d], e_in[d - 1], 1, 0)
    for j in range(4):
        rs_out[j, 0:8] = part_l[8 * j:8 * j + 8]
        rs_out[4 + j, 0:8] = part_r[8 * j:8 * j + 8]
    zero = jnp.zeros((6, TILE), F32)
    for j in range(GROUPS):
        rs_out[j, 8:16] = jnp.concatenate([mine[j:j + 1], mine[8 + j:9 + j], zero], axis=0)

    g_c = [
        remote(
            rs_out.at[lax.rem(g + d, GROUPS)], rs_in.at[d - 1], g_ss.at[d - 1], g_rs.at[d - 1], (group_at(d), b)
        )
        for d in (5, 3, 4, 6, 2, 7, 1)
    ]
    for c in g_c:
        c.start()
    for d in (1, 2, 3):
        c_out[d - 1] = cols_b[d]
    c_c = [
        remote(c_out.at[d - 1], c_in.at[d - 1], c_ss.at[d - 1], c_rs.at[d - 1], (row_at(d), b)) for d in (3, 2, 1)
    ]
    for c in c_c:
        c.start()
    mine = rs_out[g]
    for c in g_c:
        c.wait_recv()
    for d in range(GROUPS - 1):
        mine = mine + rs_in[d]
    zbuf[z] = mine.astype(BF16)

    z_c = [
        remote(
            zbuf.at[z], zbuf.at[z], z_ss.at[d - 1], z_rs.at[z], (ring_at(d), b)
        )
        for d in (8, 7, 9, 6, 10, 5, 11, 4, 12, 3, 13, 2, 14, 1, 15)
    ]
    for c in z_c:
        c.start()

    for c in c_c:
        c.wait_recv()
    col_tot = cols[0]
    for d in (1, 2, 3):
        col_tot = col_tot + c_in[d - 1].astype(F32)
    both_t = jnp.transpose(jnp.concatenate([row_tot, col_tot], axis=0)).astype(BF16)
    w_both = jnp.concatenate([wl[share, :], wr[share, :]], axis=1)
    gemb[...] = bdot(both_t, w_both, 1, 1).astype(BF16)

    for d in range(1, RING):
        at_z = lax.rem(z + d, RING)
        remote(zbuf.at[z], zbuf.at[at_z], z_ss.at[d - 1], z_rs.at[at_z], (ring_at(d), b)).wait_recv()
    whole = zbuf[0].astype(F32)
    for d in range(1, RING):
        whole = whole + zbuf[d].astype(F32)
    me = g * BAND + b
    fin[me] = whole.astype(BF16)

    order = [(d, e) for d in range(GROUPS) for e in range(BAND) if d or e]
    f_c = []
    for n, (d, e) in enumerate(order):
        f_c.append(remote(fin.at[me], fin.at[me], f_ss.at[n], f_rs.at[me], (group_at(d), band_at(e))))
    for c in f_c:
        c.start()
    for n, (d, e) in enumerate(order):
        src = lax.rem(g + d, GROUPS) * BAND + band_at(e)
        remote(fin.at[me], fin.at[src], f_ss.at[n], f_rs.at[src], (group_at(d), band_at(e))).wait_recv()
    for j in range(GROUPS):
        out = gl if j < 4 else gr
        for e in range(BAND):
            chunk = fin[j * BAND + e].astype(F32)
            out[8 * (j % 4):8 * (j % 4) + 8, TILE * e:TILE * (e + 1)] = chunk[0:8]
            gin[8 * e + j:8 * e + j + 1, :] = chunk[8:9]
            if e == 0:
                small[j:j + 1, :] = chunk[9:10]
    ar_row = small[5:6, :] * (0.5 * ALPHA)
    ar_8 = jnp.where(row_id == 0, jnp.broadcast_to(ar_row, (8, TILE)), 0.0)
    ar_col = jnp.transpose(jnp.broadcast_to(ar_row, (TILE, TILE)))
    gout[...] = ar_col[:, :CH] * wh
    gex[...] = small[...]
    gex[4:5, 0:CH] = small[4:5, 0:CH] + hdot(ar_8, wout[...].astype(F32), 1, 0)[0:1]

    for c in pay_c + e_c + x_c + s_c + g_c + c_c + z_c + f_c:
        c.wait_send()


def on_device(emb, wl, wr, win, wout, whead, dbias, offsets, vbins, target):
    vm = pl.BlockSpec(memory_space=pltpu.VMEM)
    sd = jax.ShapeDtypeStruct
    dma = pltpu.SemaphoreType.DMA
    outs = pl.pallas_call(
        kernel,
        out_shape=(
            sd((TILE, TILE), BF16), sd((TILE, TILE), BF16), sd((CH, 512), F32), sd((CH, 512), F32),
            sd((CH, HID), F32), sd((HID, CH), F32), sd((8, TILE), F32),
        ),
        in_specs=[pl.BlockSpec(memory_space=pltpu.SMEM)] + [vm] * 9,
        out_specs=(vm,) * 7,
        scratch_shapes=[
            pltpu.VMEM((HID, TILE, TILE), F32),
            pltpu.VMEM((HID, TILE, TILE), BF16),
            pltpu.VMEM((HID, TILE, TILE), BF16),
            pltpu.VMEM((HID, TILE), F32),
            pltpu.VMEM((HID, TILE), F32),
            pltpu.VMEM((HID, TILE), F32),
            pltpu.VMEM((HID, TILE), F32),
            pltpu.VMEM((HID, TILE), F32),
            pltpu.VMEM((48, TILE), BF16),
            pltpu.VMEM((3, 48, TILE), BF16),
            pltpu.VMEM((3, TILE, TILE), BF16),
            pltpu.VMEM((2 * CH, TILE), BF16),
            pltpu.VMEM((3, 2 * CH, TILE), BF16),
            pltpu.VMEM((BAND, 16, TILE), F32),
            pltpu.VMEM((3, 16, TILE), F32),
            pltpu.VMEM((8, TILE), F32),
            pltpu.VMEM((GROUPS, 16, TILE), F32),
            pltpu.VMEM((GROUPS - 1, 16, TILE), F32),
            pltpu.VMEM((RING, 16, TILE), BF16),
            pltpu.VMEM((GROUPS * BAND, 16, TILE), BF16),
            pltpu.VMEM((3, CH, TILE), BF16),
            pltpu.VMEM((3, CH, TILE), BF16),
            dma((3,)), dma((3,)), dma((3,)), dma((3,)), dma((3,)), dma((3,)), dma((3,)), dma((3,)),
            dma((7,)), dma((7,)), dma((15,)), dma((16,)), dma((31,)), dma((32,)), dma((3,)), dma((3,)),
        ],
        compiler_params=pltpu.CompilerParams(
            collective_id=0, has_side_effects=True, vmem_limit_bytes=48 * 1024 * 1024
        ),
        name="step",
    )(
        offsets, emb, wl, wr, win, wout, whead.reshape(1, CH), dbias, vbins.reshape(1, TILE),
        target.reshape(TILE, TILE),
    )
    pred, gemb, gl, gr, gin, gout, gex = outs
    return (
        pred.reshape(1, 1, TILE, TILE), gemb, gl.T, gr.T, gin, gout, gex[4, :CH], gex[:NOFF, :CH].T,
    )


def solution(mesh):
    return jax.shard_map(
        on_device,
        mesh=mesh,
        in_specs=(
            P("rows", None), P(), P(), P(), P(), P(), P(), P("rows", "band"), P("rows"),
            P("rows", "band", None, None),
        ),
        out_specs=(P("rows", "band", None, None), P("rows", "band"), P(), P(), P(), P(), P(), P()),
        check_vma=False,
    )
```

time: 278 us -> 64.2 us (0.23)
  blocking collectives: 199 us -> 0 us
  Pallas kernels: 0 us -> 55.3 us
  starting transfers between devices: 28.8 us -> 0 us
  matrix products: 25.9 us -> 0 us
  waiting for transfers between devices: 14.3 us -> 0 us
  local copies, waits for them, and re-layouts: 2.83 us -> 7.27 us
  other arithmetic: 4.02 us -> 0 us
    psum x4 -> x0, blocking collectives: 172 us -> none  [the longest x1 114 us: on_device(): lax.psum((in_part, out_part, head_part, bias_part), ROWS_BAND)]
    pallas_call x0 -> x1, Pallas kernels: none -> 55.3 us  [on_device(): pl.pallas_call(kernel, out_shape=(sd((TILE, TILE), BF16), sd((TILE, TILE)...]
    all_gather x1 -> x0, blocking collectives: 27.2 us -> none  [side_by_side(): lax.all_gather(both, axis, axis=dim, tiled=True)]
    dot_general x22 -> x0, matrix products: 25.9 us -> none  [the longest x2 7.13 us: block_terms(): lax.dot_general(w_out, grad_low, (((1,), (0,)), ((), ())), preferred_elem...]
    ppermute x9 -> x0, starting transfers between devices: 24.7 us -> none  [from_behind(): lax.ppermute(value, axis, [(source, source + steps) for source in range(l...]
    ppermute x9 -> x0, waiting for transfers between devices: 9.81 us -> none  [from_behind(): lax.ppermute(value, axis, [(source, source + steps) for source in range(l...]
    unnamed x12 -> x26, local copies, waits for them, and re-layouts: 1.3 us -> 6.18 us
    all_to_all x1 -> x0, waiting for transfers between devices: 4.48 us -> none  [copy_for_each(): lax.all_to_all(jnp.broadcast_to(array[None], (devices, *array.shape)), ax...]
  transfers between devices with their start and end apart: 10 -> 0, of which waited for: 4 -> 0; matrix products, arithmetic and copies ran while one was open for 2% -> 0% of each run, Pallas kernels for 0% -> 0%
where the time goes in v1:
time: 64.2 us; the launch traced here: 63.9 us
  Pallas kernels  55.3 us (86%)
  local copies, waits for them, and re-layouts  7.27 us (11%)
  between operations  1.35 us (2%)
    pallas_call x1, Pallas kernels, on_device(): pl.pallas_call(kernel, out_shape=(sd((TILE, TILE), BF16), sd((TILE, TILE)...  55.3 us
    unnamed x26, local copies, waits for them, and re-layouts  6.18 us

profile of v1, /device:TPU:1, one launch (start us, length us, event | category | flops | bytes accessed | tf_op | source)
XLA Modules:
  0.0 63.9 jit_solution(4606756434530159532)
XLA Ops:
  0.6 0.0 copy-start.7
  1.3 0.0 copy-start.5
  1.3 0.8 %copy.21.dbias = f32[32,4]{1,0:T(8,128)S(1)} copy(f32[32,4]{0,1:T(4,128)} %param.16) | data formatting | bytes 1024 | tf_op args[6]
  2.1 0.0 copy-done.7
  2.1 0.1 copy.20.wout
  2.2 0.0 copy-done.5
  2.2 0.0 copy-start.6
  2.2 0.0 copy-start
  2.2 0.1 copy.18.wl
  2.4 0.6 copy-done.6
  3.0 0.0 copy-start.1
  3.0 0.0 copy-start.2
  3.0 0.0 copy-start.3
  3.0 0.0 copy-start.4
  3.0 0.1 copy.19.wr
  3.1 0.0 copy-done
  3.1 0.6 copy-done.1
  3.7 0.0 copy-done.2
  3.7 0.0 copy-done.3
  3.8 0.0 copy-done.4
  3.8 55.3 %step.1 = (bf16[128,128]{1,0:T(8,128)(2,1)S(1)}, bf16[128,128]{1,0:T(8,128)(2,1)S(1)}, f32[32,512]{1,0:T(8,128)S(1)}, f32[32,512]{1,0:T(8,128)S(1)}, f32[32,128]...) custom-call(s32[1,1]{1,0:T(1,128)S(6)} %copy.28.off_ref, bf16[128,512]{1,0:T(8,128)(2,1)S(1)} %copy-done, ...), custom_call_target="tpu_custom_call" | custom-call | tf_op jit(solution)/shard_map/step/pallas_call | solution.py:326
  59.0 0.5 slice_bitcast_fusion.1
  59.5 0.6 slice_bitcast_fusion
  60.1 0.7 %copy.22 = f32[128,32]{0,1:T(8,128)} copy(f32[128,32]{1,0:T(8,128)S(1)} %get-tuple-element.27) | data formatting | bytes 32768
  60.8 0.6 copy.29
  61.4 0.6 copy.30
  62.0 0.6 copy.31
  62.6 0.6 copy.32
  63.3 0.6 copy.33
Async XLA Ops:
  0.6 1.4 %copy-start.7 = (bf16[128,32]{0,1:T(8,128)(2,1)S(1)}, bf16[128,32]{0,1:T(8,128)(2,1)}, u32[]{:S(2)}) copy-start(bf16[128,32]{0,1:T(8,128)(2,1)} %param.14) | copy-start | bytes 24580
  1.3 0.9 %copy-start.5 = (bf16[512,32]{0,1:T(8,128)(2,1)S(1)}, bf16[512,32]{0,1:T(8,128)(2,1)}, u32[]{:S(2)}) copy-start(bf16[512,32]{0,1:T(8,128)(2,1)} %param.11) | copy-start | bytes 98308
  2.2 0.8 %copy-start.6 = (bf16[512,32]{0,1:T(8,128)(2,1)S(1)}, bf16[512,32]{0,1:T(8,128)(2,1)}, u32[]{:S(2)}) copy-start(bf16[512,32]{0,1:T(8,128)(2,1)} %param.12) | copy-start | bytes 98308
  2.2 0.9 %copy-start = (bf16[128,512]{1,0:T(8,128)(2,1)S(1)}, bf16[128,512]{1,0:T(8,128)(2,1)}, u32[]{:S(2)}) copy-start(bf16[128,512]{1,0:T(8,128)(2,1)} %emb.1) | copy-start | bytes 393220
  3.0 0.8 %copy-start.1 = (bf16[1,1,128,128]{3,2,1,0:T(8,128)(2,1)S(1)}, bf16[1,1,128,128]{3,2,1,0:T(8,128)(2,1)}, u32[]{:S(2)}) copy-start(bf16[1,1,128,128]{3,2,1,0:T(8,128)(2,1)} %param.19) | copy-start | bytes 98308
  3.0 0.8 %copy-start.2 = (bf16[32,128]{1,0:T(8,128)(2,1)S(1)}, bf16[32,128]{1,0:T(8,128)(2,1)}, u32[]{:S(2)}) copy-start(bf16[32,128]{1,0:T(8,128)(2,1)} %win.1) | copy-start | bytes 24580
  3.0 0.8 %copy-start.3 = (f32[32]{0:T(128)S(1)}, f32[32]{0:T(128)}, u32[]{:S(2)}) copy-start(f32[32]{0:T(128)} %param.15) | copy-start | bytes 388
  3.0 0.8 %copy-start.4 = (s32[128]{0:T(128)S(1)}, s32[128]{0:T(128)}, u32[]{:S(2)}) copy-start(s32[128]{0:T(128)} %param.18) | copy-start | bytes 1540

commit v2 on v1

--- a/solution.py
+++ b/solution.py
@@ -36,14 +36,27 @@
 
 
 def kernel(
-    off_ref, emb, wl, wr, win, wout, whead, dbias, vbins, tgt,
-    pred, gemb, gl, gr, gin, gout, gex,
+    emb_h, wl_h, wr_h, win_h, wout_h, whead_h, dbias_h, off_h, vbins_h, tgt_h,
+    pred, gemb, gl, gr, gin, gout, ghead, gbias,
+    emb, wl, wr, win, wout, whead, dbias, off, vbins, tgt, load_s,
     abc, act, slope, b_s, v_s, gr_s, gc_s, ar_s,
     pay, pay_in, e_in,
     x_out, x_in, s_out, s_in, small,
     rs_out, rs_in, zbuf, fin, c_out, c_in,
-    pay_ss, pay_rs, e_ss, e_rs, x_ss, x_rs, s_ss, s_rs, g_ss, g_rs, z_ss, z_rs, f_ss, f_rs, c_ss, c_rs,
+    pay_ss, pay_rs, e_ss, e_rs, x_ss, x_rs, s_ss, s_rs, g_ss, g_rs, z_ss, z_rs, f_ss, f_rs, c_ss, c_rs, here,
 ):
+    loads = [
+        pltpu.make_async_copy(src, dst, load_s.at[n])
+        for n, (src, dst) in enumerate(
+            [
+                (wr_h, wr), (emb_h, emb), (wl_h, wl), (vbins_h, vbins), (win_h, win), (wout_h, wout),
+                (whead_h, whead), (dbias_h, dbias), (off_h, off), (tgt_h, tgt),
+            ]
+        )
+    ]
+    for c in loads:
+        c.start()
+
     r = lax.axis_index("rows")
     b = lax.axis_index("band")
     z = lax.rem(r, RING)
@@ -69,18 +82,17 @@
 
     barrier = pltpu.get_barrier_semaphore()
     partners = [(row_at(d), b) for d in (-3, -2, -1, 1, 2, 3)]
-    partners += [(ring_at(d), b) for d in range(1, RING)]
+    partners += [(ring_at(d), b) for d in (1, 2, 3, 4, 12, 13, 14, 15)]
     partners += [(group_at(d), band_at(e)) for d in range(GROUPS) for e in range(BAND) if d or e]
     for dev in partners:
         pl.semaphore_signal(barrier, inc=1, device_id=dev, device_id_type=MESH)
 
-    lt = bdot(emb[...], wl[...], 1, 0).astype(BF16)
-    rt = bdot(emb[...], wr[...], 1, 0).astype(BF16)
-    ltf, rtf = lt.astype(F32), rt.astype(F32)
-    lr = jnp.transpose(jnp.concatenate([ltf, rtf], axis=1))
-    left, right = lr[:CH], lr[CH:]
+    for c in loads[:4]:
+        c.wait()
+    right_b = bdot(wr[...], emb[...], 1, 1).astype(BF16)
+    right = right_b.astype(F32)
     flags = vbins[...].astype(F32)
-    pay[0:CH] = right.astype(BF16)
+    pay[0:CH] = right_b
     pay[CH:CH + 16] = jnp.broadcast_to(flags, (16, TILE)).astype(BF16)
 
     pl.semaphore_wait(barrier, len(partners))
@@ -89,8 +101,15 @@
     ]
     for c in pay_c:
         c.start()
+    for d in (4, 12):
+        pl.semaphore_signal(here, inc=1, device_id=(ring_at(d), b), device_id_type=MESH)
 
     share = pl.ds(pl.multiple_of(b * TILE, TILE), TILE)
+    left = bdot(wl[...], emb[...], 1, 1).astype(BF16).astype(F32)
+    ltf = jnp.transpose(left)
+    lt = ltf.astype(BF16)
+    for c in loads[4:]:
+        c.wait()
     wh = whead[...]
     wcol = jnp.sum(
         jnp.where(
@@ -98,8 +117,9 @@
         ),
         axis=1, keepdims=True,
     )
-    v_s[...] = jnp.broadcast_to(
-        jnp.sum(wout[...].astype(F32) * wh, axis=1, keepdims=True), (HID, TILE)
+    wout_f = wout[...].astype(F32)
+    v_s[...] = jnp.transpose(
+        jnp.broadcast_to(jnp.sum(wout_f * wcol, axis=0, keepdims=True), (TILE, HID))
     )
     row_logit = jnp.sum(ltf * wh, axis=1, keepdims=True)
     win_f = win[...].astype(F32)
@@ -113,10 +133,14 @@
 
     lax.fori_loop(0, HID // 8, spread, at)
 
-    offset = off_ref[0, 0]
+    offset = off[...]
     hot = [jnp.where(offset == j, 1.0, 0.0).astype(F32) for j in range(NOFF)]
+    bias_row = sum(dbias[j:j + 1, :] * hot[j] for j in range(NOFF))
     bias_col = jnp.sum(
-        jnp.where(lax.broadcasted_iota(jnp.int32, (CH, NOFF), 1) == offset, dbias[...], 0.0),
+        jnp.where(
+            lax.broadcasted_iota(jnp.int32, (CH, CH), 0) == lax.broadcasted_iota(jnp.int32, (CH, CH), 1),
+            bias_row, 0.0,
+        ),
         axis=1, keepdims=True,
     )
 
@@ -140,19 +164,19 @@
     col_logit = jnp.sum(r_b * wcol, axis=0, keepdims=True)
 
     def first(i, total):
-        for j in range(4):
-            k = 4 * i + j
+        for j in range(8):
+            k = 8 * i + j
             y = abc[k] + b_s[pl.ds(k, 1), :]
             w = y * y + BETA
             t = jnp.tanh(y * w)
             q = 1.0 + t
             a2 = y * q
-            act[k] = a2.astype(BF16)
-            slope[k] = (q + (a2 * (1.0 - t)) * (3.0 * w - 2.0 * BETA)).astype(BF16)
+            act[k] = a2
+            slope[k] = q + (a2 * (1.0 - t)) * (3.0 * w - 2.0 * BETA)
             total = total + a2 * v_s[pl.ds(k, 1), :]
         return total
 
-    total = lax.fori_loop(0, HID // 4, first, jnp.zeros((TILE, TILE), F32))
+    total = lax.fori_loop(0, HID // 8, first, jnp.zeros((TILE, TILE), F32))
     logits = total * (0.5 * ALPHA) + (row_logit + col_logit)
     pred[...] = logits.astype(BF16)
     row_flags = jnp.sum(
@@ -163,21 +187,22 @@
         axis=1, keepdims=True,
     )
     res = (row_flags * f_sel) * (logits - tgt[...].astype(F32)) * (1.0 / (NOFF * TILE))
-    res_b = res.astype(BF16)
     ones = jnp.ones((8, TILE), BF16)
 
     def second(i, carry):
-        for j in range(4):
-            k = 4 * i + j
-            h = slope[k] * res_b
-            a = act[k] * res_b
-            both = bdot(ones, jnp.concatenate([h, a], axis=1), 1, 0)
-            gc_s[pl.ds(k, 1), :] = both[0:1, :TILE]
-            ar_s[pl.ds(k, 1), :] = both[0:1, TILE:]
-            gr_s[pl.ds(k, 1), :] = bdot(ones, h, 1, 1)[0:1]
+        parts = []
+        for j in range(16):
+            k = 16 * i + j
+            h = slope[k] * res
+            gc_s[pl.ds(k, 1), :] = jnp.sum(h, axis=0, keepdims=True)
+            ar_s[pl.ds(k, 1), :] = jnp.sum(act[k] * res, axis=0, keepdims=True)
+            parts.append(h.astype(BF16))
+        over_q = bdot(ones, jnp.concatenate(parts, axis=0), 1, 1)
+        for j in range(16):
+            gr_s[pl.ds(16 * i + j, 1), :] = over_q[0:1, TILE * j:TILE * (j + 1)]
         return carry
 
-    lax.fori_loop(0, HID // 4, second, 0)
+    lax.fori_loop(0, HID // 16, second, 0)
 
     ones_f = jnp.ones((8, TILE), F32)
     half_v = v_s[...] * 0.5
@@ -264,6 +289,7 @@
         mine = mine + rs_in[d]
     zbuf[z] = mine.astype(BF16)
 
+    pl.semaphore_wait(here, 2)
     z_c = [
         remote(
             zbuf.at[z], zbuf.at[z], z_ss.at[d - 1], z_rs.at[z], (ring_at(d), b)
@@ -279,8 +305,8 @@
     for d in (1, 2, 3):
         col_tot = col_tot + c_in[d - 1].astype(F32)
     both_t = jnp.transpose(jnp.concatenate([row_tot, col_tot], axis=0)).astype(BF16)
-    w_both = jnp.concatenate([wl[share, :], wr[share, :]], axis=1)
-    gemb[...] = bdot(both_t, w_both, 1, 1).astype(BF16)
+    w_both = jnp.concatenate([wl[:, share], wr[:, share]], axis=0)
+    gemb[...] = bdot(both_t, w_both, 1, 0).astype(BF16)
 
     for d in range(1, RING):
         at_z = lax.rem(z + d, RING)
@@ -309,32 +335,52 @@
             if e == 0:
                 small[j:j + 1, :] = chunk[9:10]
     ar_row = small[5:6, :] * (0.5 * ALPHA)
-    ar_8 = jnp.where(row_id == 0, jnp.broadcast_to(ar_row, (8, TILE)), 0.0)
-    ar_col = jnp.transpose(jnp.broadcast_to(ar_row, (TILE, TILE)))
-    gout[...] = ar_col[:, :CH] * wh
-    gex[...] = small[...]
-    gex[4:5, 0:CH] = small[4:5, 0:CH] + hdot(ar_8, wout[...].astype(F32), 1, 0)[0:1]
+    gout[...] = wcol * ar_row
+    ghead[...] = small[4:5, 0:CH] + hdot(jnp.broadcast_to(ar_row, (8, TILE)), wout_f, 1, 1)[0:1]
+    gbias[...] = small[0:NOFF, 0:CH]
 
     for c in pay_c + e_c + x_c + s_c + g_c + c_c + z_c + f_c:
         c.wait_send()
 
 
+def write_out(*refs):
+    n = (len(refs) - 1) // 2
+    copies = [pltpu.make_async_copy(refs[i], refs[n + i], refs[-1].at[i]) for i in range(n)]
+    for c in copies:
+        c.start()
+    for c in copies:
+        c.wait()
+
+
 def on_device(emb, wl, wr, win, wout, whead, dbias, offsets, vbins, target):
     vm = pl.BlockSpec(memory_space=pltpu.VMEM)
+    hbm = pl.BlockSpec(memory_space=pltpu.HBM)
     sd = jax.ShapeDtypeStruct
     dma = pltpu.SemaphoreType.DMA
+    out_shape = (
+        sd((TILE, TILE), BF16), sd((TILE, TILE), BF16), sd((CH, 512), F32), sd((CH, 512), F32),
+        sd((CH, HID), F32), sd((CH, HID), F32), sd((1, CH), F32), sd((NOFF, CH), F32),
+    )
     outs = pl.pallas_call(
         kernel,
-        out_shape=(
-            sd((TILE, TILE), BF16), sd((TILE, TILE), BF16), sd((CH, 512), F32), sd((CH, 512), F32),
-            sd((CH, HID), F32), sd((HID, CH), F32), sd((8, TILE), F32),
-        ),
-        in_specs=[pl.BlockSpec(memory_space=pltpu.SMEM)] + [vm] * 9,
-        out_specs=(vm,) * 7,
+        out_shape=out_shape,
+        in_specs=[hbm] * 10,
+        out_specs=(vm,) * 8,
         scratch_shapes=[
+            pltpu.VMEM((TILE, 512), BF16),
+            pltpu.VMEM((CH, 512), BF16),
+            pltpu.VMEM((CH, 512), BF16),
+            pltpu.VMEM((CH, HID), BF16),
+            pltpu.VMEM((CH, HID), BF16),
+            pltpu.VMEM((1, CH), F32),
+            pltpu.VMEM((NOFF, CH), F32),
+            pltpu.VMEM((1, 1), jnp.int32),
+            pltpu.VMEM((1, TILE), jnp.int32),
+            pltpu.VMEM((TILE, TILE), BF16),
+            dma((10,)),
             pltpu.VMEM((HID, TILE, TILE), F32),
-            pltpu.VMEM((HID, TILE, TILE), BF16),
-            pltpu.VMEM((HID, TILE, TILE), BF16),
+            pltpu.VMEM((HID, TILE, TILE), F32),
+            pltpu.VMEM((HID, TILE, TILE), F32),
             pltpu.VMEM((HID, TILE), F32),
             pltpu.VMEM((HID, TILE), F32),
             pltpu.VMEM((HID, TILE), F32),
@@ -356,18 +402,27 @@
             pltpu.VMEM((3, CH, TILE), BF16),
             dma((3,)), dma((3,)), dma((3,)), dma((3,)), dma((3,)), dma((3,)), dma((3,)), dma((3,)),
             dma((7,)), dma((7,)), dma((15,)), dma((16,)), dma((31,)), dma((32,)), dma((3,)), dma((3,)),
+            pltpu.SemaphoreType.REGULAR,
         ],
         compiler_params=pltpu.CompilerParams(
             collective_id=0, has_side_effects=True, vmem_limit_bytes=48 * 1024 * 1024
         ),
         name="step",
     )(
-        offsets, emb, wl, wr, win, wout, whead.reshape(1, CH), dbias, vbins.reshape(1, TILE),
+        emb, wl.T, wr.T, win, wout.T, whead.reshape(1, CH), dbias.T, offsets, vbins.reshape(1, TILE),
         target.reshape(TILE, TILE),
     )
-    pred, gemb, gl, gr, gin, gout, gex = outs
+    pred, gemb, gl, gr, gin, gout, ghead, gbias = pl.pallas_call(
+        write_out,
+        out_shape=out_shape,
+        in_specs=[vm] * 8,
+        out_specs=(hbm,) * 8,
+        scratch_shapes=[dma((8,))],
+        compiler_params=pltpu.CompilerParams(vmem_limit_bytes=1024 * 1024),
+        name="write_out",
+    )(*outs)
     return (
-        pred.reshape(1, 1, TILE, TILE), gemb, gl.T, gr.T, gin, gout, gex[4, :CH], gex[:NOFF, :CH].T,
+        pred.reshape(1, 1, TILE, TILE), gemb, gl.T, gr.T, gin, gout.T, ghead.reshape(CH), gbias.T,
     )
 
 

time: 64.2 us -> 58.5 us (0.911)
  Pallas kernels: 55.3 us -> 52.1 us
  local copies, waits for them, and re-layouts: 7.27 us -> 4.53 us
    pallas_call x1 -> x2, Pallas kernels: 55.3 us -> 52.1 us  [the longest x1 51.4 us: on_device(): pl.pallas_call(kernel, out_shape=out_shape, in_specs=[hbm] * 10, out_spec...]
    unnamed x26 -> x18, local copies, waits for them, and re-layouts: 6.18 us -> 4.53 us
where the time goes in v2:
time: 58.5 us; the launch traced here: 58 us
  Pallas kernels  52.1 us (89%)
  local copies, waits for them, and re-layouts  4.53 us (8%)
  between operations  1.35 us (2%)
    pallas_call x1, Pallas kernels, on_device(): pl.pallas_call(kernel, out_shape=out_shape, in_specs=[hbm] * 10, out_spec...  51.4 us
    unnamed x18, local copies, waits for them, and re-layouts  4.53 us

profile of v2, /device:TPU:1, one launch (start us, length us, event | category | flops | bytes accessed | tf_op | source)
XLA Modules:
  0.0 58.0 jit_solution(17827589219100850580)
XLA Ops:
  0.6 0.0 copy-start.4
  1.3 0.0 copy-start.6
  1.3 0.0 copy-start.7
  1.3 0.0 copy-start.8
  1.3 0.0 copy-done.4
  1.3 0.6 %copy-done.6 = f32[32,4]{0,1:T(4,128)S(1)} copy-done((f32[32,4]{0,1:T(4,128)S(1)}, f32[32,4]{0,1:T(4,128)}, u32[]{:S(2)}) %copy-start.6) | copy-done | bytes 536
  2.0 0.0 copy-done.7
  2.0 0.0 copy-done.8
  2.0 0.0 copy-start
  2.0 0.9 %copy-done = bf16[128,512]{1,0:T(8,128)(2,1)S(1)} copy-done((bf16[128,512]{1,0:T(8,128)(2,1)S(1)}, bf16[128,512]{1,0:T(8,128)(2,1)}, u32[]{:S(2)}) %copy-start) | copy-done | bytes 131096
  2.9 0.0 copy-start.1
  2.9 0.8 %copy-done.1 = bf16[512,32]{0,1:T(8,128)(2,1)S(1)} copy-done((bf16[512,32]{0,1:T(8,128)(2,1)S(1)}, bf16[512,32]{0,1:T(8,128)(2,1)}, u32[]{:S(2)}) %copy-start.1) | copy-done | bytes 32792
  3.7 0.0 copy-start.2
  3.7 0.8 %copy-done.2 = bf16[512,32]{0,1:T(8,128)(2,1)S(1)} copy-done((bf16[512,32]{0,1:T(8,128)(2,1)S(1)}, bf16[512,32]{0,1:T(8,128)(2,1)}, u32[]{:S(2)}) %copy-start.2) | copy-done | bytes 32792
  4.4 0.0 copy-start.3
  4.4 0.8 %copy-done.3 = bf16[1,1,128,128]{3,2,1,0:T(8,128)(2,1)S(1)} copy-done((bf16[1,1,128,128]{3,2,1,0:T(8,128)(2,1)S(1)}, bf16[1,1,128,128]{3,2,1,0:T(8,128)(2,1)}, u32[]{:S(2)}) %copy-start.3) | copy-done | bytes 32792
  5.2 0.0 copy-start.5
  5.2 0.7 %copy-done.5 = bf16[128,32]{0,1:T(8,128)(2,1)S(1)} copy-done((bf16[128,32]{0,1:T(8,128)(2,1)S(1)}, bf16[128,32]{0,1:T(8,128)(2,1)}, u32[]{:S(2)}) %copy-start.5) | copy-done | bytes 8216
  5.9 51.4 %step.1 = (bf16[128,128]{1,0:T(8,128)(2,1)S(1)}, bf16[128,128]{1,0:T(8,128)(2,1)S(1)}, f32[32,512]{1,0:T(8,128)S(1)}, f32[32,512]{1,0:T(8,128)S(1)}, f32[32,128]...) custom-call(bf16[128,512]{1,0:T(8,128)(2,1)S(1)} %copy-done, ...), custom_call_target="tpu_custom_call" | custom-call | tf_op jit(solution)/shard_map/step/pallas_call | solution.py:364
  57.3 0.8 %write_out.1 = (bf16[128,128]{1,0:T(8,128)(2,1)}, bf16[128,128]{1,0:T(8,128)(2,1)}, f32[32,512]{1,0:T(8,128)}, f32[32,512]{1,0:T(8,128)}, f32[32,128]{1,0:T(8,12...) custom-call(bf16[128,128]{1,0:T(8,128)(2,1)S(1)} %get-tuple-element.24.refs_0_, ...), custom_call_target="tpu_custom_call" | custom-call | tf_op jit(solution)/shard_map/write_out/pallas_call | solution.py:415
Async XLA Ops:
  0.6 0.7 %copy-start.4 = (bf16[32,128]{1,0:T(8,128)(2,1)S(1)}, bf16[32,128]{1,0:T(8,128)(2,1)}, u32[]{:S(2)}) copy-start(bf16[32,128]{1,0:T(8,128)(2,1)} %win_h.1) | copy-start | bytes 24580
  1.3 0.7 %copy-start.6 = (f32[32,4]{0,1:T(4,128)S(1)}, f32[32,4]{0,1:T(4,128)}, u32[]{:S(2)}) copy-start(f32[32,4]{0,1:T(4,128)} %param.16) | copy-start | bytes 1540
  1.3 0.7 %copy-start.7 = (f32[32]{0:T(128)S(1)}, f32[32]{0:T(128)}, u32[]{:S(2)}) copy-start(f32[32]{0:T(128)} %param.15) | copy-start | bytes 388
  1.3 0.7 %copy-start.8 = (s32[128]{0:T(128)S(1)}, s32[128]{0:T(128)}, u32[]{:S(2)}) copy-start(s32[128]{0:T(128)} %param.18) | copy-start | bytes 1540
  2.0 0.9 %copy-start = (bf16[128,512]{1,0:T(8,128)(2,1)S(1)}, bf16[128,512]{1,0:T(8,128)(2,1)}, u32[]{:S(2)}) copy-start(bf16[128,512]{1,0:T(8,128)(2,1)} %emb_h.1) | copy-start | bytes 393220
  2.9 0.8 %copy-start.1 = (bf16[512,32]{0,1:T(8,128)(2,1)S(1)}, bf16[512,32]{0,1:T(8,128)(2,1)}, u32[]{:S(2)}) copy-start(bf16[512,32]{0,1:T(8,128)(2,1)} %param.11) | copy-start | bytes 98308
  3.7 0.8 %copy-start.2 = (bf16[512,32]{0,1:T(8,128)(2,1)S(1)}, bf16[512,32]{0,1:T(8,128)(2,1)}, u32[]{:S(2)}) copy-start(bf16[512,32]{0,1:T(8,128)(2,1)} %param.12) | copy-start | bytes 98308
  4.4 0.8 %copy-start.3 = (bf16[1,1,128,128]{3,2,1,0:T(8,128)(2,1)S(1)}, bf16[1,1,128,128]{3,2,1,0:T(8,128)(2,1)}, u32[]{:S(2)}) copy-start(bf16[1,1,128,128]{3,2,1,0:T(8,128)(2,1)} %param.19) | copy-start | bytes 98308
  5.2 0.7 %copy-start.5 = (bf16[128,32]{0,1:T(8,128)(2,1)S(1)}, bf16[128,32]{0,1:T(8,128)(2,1)}, u32[]{:S(2)}) copy-start(bf16[128,32]{0,1:T(8,128)(2,1)} %param.14) | copy-start | bytes 24580

commit v3 on v2

--- a/solution.py
+++ b/solution.py
@@ -15,6 +15,16 @@
 RING = 16
 GROUPS = 8
 BAND = 4
+GROUP_OFFSETS = ((2, 1), (2, 0), (1, 1), (3, 1), (1, 0), (3, 0), (0, 1))
+BAND_OFFSETS = ((1, 1), (1, 0), (0, 1))
+ALL_OFFSETS = sorted(
+    (
+        (dy, dx, dh, dc)
+        for dy in range(4) for dx in range(2) for dh in range(2) for dc in range(2)
+        if dy or dx or dh or dc
+    ),
+    key=lambda o: (-min(o[0], 4 - o[0]) - (1 if o[1] else 2 * o[2]), -o[3]),
+)
 MESH = pl.DeviceIdType.MESH
 F32 = jnp.float32
 BF16 = jnp.bfloat16
@@ -35,57 +45,72 @@
     return lax.dot_general(a, b, (((ca,), (cb,)), ((), ())), preferred_element_type=F32)
 
 
+def halves(x):
+    hi = x.astype(BF16)
+    return hi, (x - hi.astype(F32)).astype(BF16)
+
+
 def kernel(
     emb_h, wl_h, wr_h, win_h, wout_h, whead_h, dbias_h, off_h, vbins_h, tgt_h,
     pred, gemb, gl, gr, gin, gout, ghead, gbias,
-    emb, wl, wr, win, wout, whead, dbias, off, vbins, tgt, load_s,
+    emb, wl, wr, win, wout, whead, dbias, vbins, tgt, load_s,
     abc, act, slope, b_s, v_s, gr_s, gc_s, ar_s,
     pay, pay_in, e_in,
     x_out, x_in, s_out, s_in, small,
     rs_out, rs_in, zbuf, fin, c_out, c_in,
-    pay_ss, pay_rs, e_ss, e_rs, x_ss, x_rs, s_ss, s_rs, g_ss, g_rs, z_ss, z_rs, f_ss, f_rs, c_ss, c_rs, here,
+    pay_ss, pay_rs, e_ss, e_rs, x_ss, x_rs, s_ss, s_rs, g_ss, g_rs, z_ss, z_rs, f_ss, f_rs, c_ss, c_rs, here, there,
 ):
+    r = lax.axis_index("rows")
+    b = lax.axis_index("band")
+    z = lax.rem(r, RING)
+    base = r - z
+    g = lax.div(r, RING)
+    gy, gx = lax.div(g, 2), lax.rem(g, 2)
+    bh, bc = lax.div(b, 2), lax.rem(b, 2)
+
+    def row_at(d):
+        return lax.rem(r + (d + ROWS), ROWS)
+
+    def ring_at(d):
+        return base + lax.rem(z + d, RING)
+
+    def group_index(dy, dx):
+        return lax.rem(gy + dy, 4) * 2 + lax.rem(gx + dx, 2)
+
+    def group_at(dy, dx):
+        return group_index(dy, dx) * RING + z
+
+    def band_at(dh, dc):
+        return lax.rem(bh + dh, 2) * 2 + lax.rem(bc + dc, 2)
+
+    def signal(sem, dev):
+        pl.semaphore_signal(sem, inc=1, device_id=dev, device_id_type=MESH)
+
+    def remote(src, dst, ss, rs, dev):
+        return pltpu.make_async_remote_copy(
+            src_ref=src, dst_ref=dst, send_sem=ss, recv_sem=rs, device_id=dev, device_id_type=MESH
+        )
+
+    barrier = pltpu.get_barrier_semaphore()
+    near = [(row_at(d), b) for d in (-3, 3, -2, 2, -1, 1)]
+    for dev in near:
+        signal(barrier, dev)
     loads = [
         pltpu.make_async_copy(src, dst, load_s.at[n])
         for n, (src, dst) in enumerate(
             [
                 (wr_h, wr), (emb_h, emb), (wl_h, wl), (vbins_h, vbins), (win_h, win), (wout_h, wout),
-                (whead_h, whead), (dbias_h, dbias), (off_h, off), (tgt_h, tgt),
+                (whead_h, whead), (dbias_h, dbias), (tgt_h, tgt),
             ]
         )
     ]
     for c in loads:
         c.start()
-
-    r = lax.axis_index("rows")
-    b = lax.axis_index("band")
-    z = lax.rem(r, RING)
-    base = r - z
-    g = lax.div(r, RING)
-
-    def row_at(d):
-        return lax.rem(r + (d + ROWS), ROWS)
-
-    def ring_at(d):
-        return base + lax.rem(z + d, RING)
-
-    def group_at(d):
-        return lax.rem(r + RING * d, ROWS)
-
-    def band_at(d):
-        return lax.rem(b + d, BAND)
-
-    def remote(src, dst, ss, rs, dev):
-        return pltpu.make_async_remote_copy(
-            src_ref=src, dst_ref=dst, send_sem=ss, recv_sem=rs, device_id=dev, device_id_type=MESH
-        )
-
-    barrier = pltpu.get_barrier_semaphore()
-    partners = [(row_at(d), b) for d in (-3, -2, -1, 1, 2, 3)]
-    partners += [(ring_at(d), b) for d in (1, 2, 3, 4, 12, 13, 14, 15)]
-    partners += [(group_at(d), band_at(e)) for d in range(GROUPS) for e in range(BAND) if d or e]
-    for dev in partners:
-        pl.semaphore_signal(barrier, inc=1, device_id=dev, device_id_type=MESH)
+    rest = [(group_at(dy, dx), b) for dy, dx in GROUP_OFFSETS]
+    rest += [(r, band_at(dh, dc)) for dh, dc in BAND_OFFSETS]
+    rest += [(ring_at(d), b) for d in (2, 14, 1, 15)]
+    for dev in rest:
+        signal(barrier, dev)
 
     for c in loads[:4]:
         c.wait()
@@ -95,14 +120,16 @@
     pay[0:CH] = right_b
     pay[CH:CH + 16] = jnp.broadcast_to(flags, (16, TILE)).astype(BF16)
 
-    pl.semaphore_wait(barrier, len(partners))
+    pl.semaphore_wait(barrier, len(near) + len(rest))
     pay_c = [
         remote(pay, pay_in.at[d - 1], pay_ss.at[d - 1], pay_rs.at[d - 1], (row_at(-d), b)) for d in (3, 2, 1)
     ]
     for c in pay_c:
         c.start()
-    for d in (4, 12):
-        pl.semaphore_signal(here, inc=1, device_id=(ring_at(d), b), device_id_type=MESH)
+    for dy, dx in GROUP_OFFSETS:
+        signal(here, (group_at(dy, dx), b))
+    for d in (2, 14):
+        signal(here, (ring_at(d), b))
 
     share = pl.ds(pl.multiple_of(b * TILE, TILE), TILE)
     left = bdot(wl[...], emb[...], 1, 1).astype(BF16).astype(F32)
@@ -111,19 +138,29 @@
     for c in loads[4:]:
         c.wait()
     wh = whead[...]
-    wcol = jnp.sum(
+    eye = lax.broadcasted_iota(jnp.int32, (CH, CH), 0) == lax.broadcasted_iota(jnp.int32, (CH, CH), 1)
+    wcol = jnp.sum(jnp.where(eye, wh, 0.0), axis=1, keepdims=True)
+    wout_f = wout[...].astype(F32)
+    win_f = win[...].astype(F32)
+    win_t = jnp.transpose(win_f)
+    v_row = jnp.sum(wout_f * wcol, axis=0, keepdims=True)
+    v_s[...] = jnp.transpose(jnp.broadcast_to(v_row, (TILE, HID)))
+    wcol_lin = wcol + 0.5 * jnp.sum(win_f * v_row, axis=1, keepdims=True)
+    wrow_lin = jnp.sum(jnp.where(eye, wcol_lin, 0.0), axis=0, keepdims=True)
+    row_logit = jnp.sum(ltf * wrow_lin, axis=1, keepdims=True)
+    offset = off_h[0, 0]
+    hot = [jnp.where(offset == j, 1.0, 0.0).astype(F32) for j in range(NOFF)]
+    bias_row = sum(dbias[j:j + 1, :] * hot[j] for j in range(NOFF))
+    bias_col = jnp.sum(jnp.where(eye, bias_row, 0.0), axis=1, keepdims=True)
+    b_s[...] = hdot(win_t, jnp.broadcast_to(bias_col, (CH, TILE)), 1, 0) * (1.0 / ALPHA)
+    row_flags = jnp.sum(
         jnp.where(
-            lax.broadcasted_iota(jnp.int32, (CH, CH), 0) == lax.broadcasted_iota(jnp.int32, (CH, CH), 1), wh, 0.0
+            lax.broadcasted_iota(jnp.int32, (TILE, TILE), 0) == lax.broadcasted_iota(jnp.int32, (TILE, TILE), 1),
+            flags, 0.0,
         ),
         axis=1, keepdims=True,
     )
-    wout_f = wout[...].astype(F32)
-    v_s[...] = jnp.transpose(
-        jnp.broadcast_to(jnp.sum(wout_f * wcol, axis=0, keepdims=True), (TILE, HID))
-    )
-    row_logit = jnp.sum(ltf * wh, axis=1, keepdims=True)
-    win_f = win[...].astype(F32)
-    win_t = jnp.transpose(win_f)
+    tgt_f = tgt[...].astype(F32)
     at = bdot(lt, win[...], 1, 0) * (1.0 / ALPHA)
 
     def spread(i, rolled):
@@ -133,16 +170,9 @@
 
     lax.fori_loop(0, HID // 8, spread, at)
 
-    offset = off[...]
-    hot = [jnp.where(offset == j, 1.0, 0.0).astype(F32) for j in range(NOFF)]
-    bias_row = sum(dbias[j:j + 1, :] * hot[j] for j in range(NOFF))
-    bias_col = jnp.sum(
-        jnp.where(
-            lax.broadcasted_iota(jnp.int32, (CH, CH), 0) == lax.broadcasted_iota(jnp.int32, (CH, CH), 1),
-            bias_row, 0.0,
-        ),
-        axis=1, keepdims=True,
-    )
+    pl.semaphore_wait(here, len(GROUP_OFFSETS) + 2)
+    for d in (4, 12):
+        signal(there, (ring_at(d), b))
 
     r_sel = right * hot[0]
     f_sel = flags * hot[0]
@@ -160,8 +190,8 @@
         c.start()
 
     r_b = r_sel + bias_col
-    b_s[...] = hdot(win_t, r_b, 1, 0) * (1.0 / ALPHA)
-    col_logit = jnp.sum(r_b * wcol, axis=0, keepdims=True)
+    b_s[...] += bdot(win_t.astype(BF16), r_sel.astype(BF16), 1, 0) * (1.0 / ALPHA)
+    col_logit = jnp.sum(r_b * wcol_lin, axis=0, keepdims=True)
 
     def first(i, total):
         for j in range(8):
@@ -169,74 +199,71 @@
             y = abc[k] + b_s[pl.ds(k, 1), :]
             w = y * y + BETA
             t = jnp.tanh(y * w)
-            q = 1.0 + t
-            a2 = y * q
-            act[k] = a2
-            slope[k] = q + (a2 * (1.0 - t)) * (3.0 * w - 2.0 * BETA)
-            total = total + a2 * v_s[pl.ds(k, 1), :]
+            yt = y * t
+            act[k] = yt
+            slope[k] = t + (y - t * yt) * (3.0 * w - 2.0 * BETA)
+            total = total + yt * v_s[pl.ds(k, 1), :]
         return total
 
     total = lax.fori_loop(0, HID // 8, first, jnp.zeros((TILE, TILE), F32))
     logits = total * (0.5 * ALPHA) + (row_logit + col_logit)
     pred[...] = logits.astype(BF16)
-    row_flags = jnp.sum(
-        jnp.where(
-            lax.broadcasted_iota(jnp.int32, (TILE, TILE), 0) == lax.broadcasted_iota(jnp.int32, (TILE, TILE), 1),
-            flags, 0.0,
-        ),
-        axis=1, keepdims=True,
-    )
-    res = (row_flags * f_sel) * (logits - tgt[...].astype(F32)) * (1.0 / (NOFF * TILE))
+    res = (row_flags * f_sel) * (logits - tgt_f) * (1.0 / (NOFF * TILE))
     ones = jnp.ones((8, TILE), BF16)
 
     def second(i, carry):
         parts = []
-        for j in range(16):
-            k = 16 * i + j
+        for j in range(32):
+            k = 32 * i + j
             h = slope[k] * res
             gc_s[pl.ds(k, 1), :] = jnp.sum(h, axis=0, keepdims=True)
             ar_s[pl.ds(k, 1), :] = jnp.sum(act[k] * res, axis=0, keepdims=True)
             parts.append(h.astype(BF16))
         over_q = bdot(ones, jnp.concatenate(parts, axis=0), 1, 1)
-        for j in range(16):
-            gr_s[pl.ds(16 * i + j, 1), :] = over_q[0:1, TILE * j:TILE * (j + 1)]
+        for j in range(32):
+            gr_s[pl.ds(32 * i + j, 1), :] = over_q[0:1, TILE * j:TILE * (j + 1)]
         return carry
 
-    lax.fori_loop(0, HID // 16, second, 0)
-
-    ones_f = jnp.ones((8, TILE), F32)
+    lax.fori_loop(0, HID // 32, second, 0)
+
     half_v = v_s[...] * 0.5
-    g_both = jnp.concatenate([gr_s[...] * half_v, gc_s[...] * half_v], axis=1)
-    rr = hdot(ones_f, res, 1, 1)
+    res_hi, res_lo = halves(res)
+    rr = bdot(jnp.ones((8, 2 * TILE), BF16), jnp.concatenate([res_hi, res_lo], axis=1), 1, 1)
     rc = jnp.broadcast_to(jnp.sum(res, axis=0, keepdims=True), (8, TILE))
     r_both = jnp.concatenate([rr, rc], axis=1)
+    g_both = jnp.concatenate([(gr_s[...] + rr[0:1]) * half_v, (gc_s[...] + rc[0:1]) * half_v], axis=1)
+    g_hi, g_lo = halves(g_both)
+    sums = wcol * r_both[0:1] + bdot(
+        jnp.concatenate([win[...], win[...]], axis=1), jnp.concatenate([g_hi, g_lo], axis=0), 1, 0
+    )
+    sums_b = sums.astype(BF16)
+
+    x_out[0:CH] = sums_b[:, :TILE]
+    x_out[CH:2 * CH] = sums_b[:, TILE:]
+    x_c, s_c = [], []
+    for n, (dh, dc) in enumerate(BAND_OFFSETS):
+        dev = (r, band_at(dh, dc))
+        x_c.append(remote(x_out, x_in.at[n], x_ss.at[n], x_rs.at[n], dev))
+        s_c.append(remote(s_out.at[band_at(dh, dc)], s_in.at[n], s_ss.at[n], s_rs.at[n], dev))
+    for c in x_c:
+        c.start()
     p_both = jnp.concatenate([left, r_b], axis=1)
-    sums = hdot(win_f, g_both, 1, 0) + wcol * r_both[0:1]
-    sums_b = sums.astype(BF16)
     gin_part = hdot(p_both, g_both, 1, 1)
     head = hdot(r_both, p_both, 1, 1)
+    ones_f = jnp.ones((8, TILE), F32)
     bias = hdot(ones_f, sums[:, :TILE], 1, 1)
-    ar = hdot(ones_f, ar_s[...], 1, 1)
+    ar = hdot(ones_f, ar_s[...], 1, 1) + hdot(head, win_f, 1, 0) * (1.0 / ALPHA)
     row_id = lax.broadcasted_iota(jnp.int32, (8, TILE), 0)
     small[...] = jnp.where(row_id == 5, ar, jnp.where(row_id == 6, offset.astype(F32), 0.0))
     for j in range(NOFF):
         small[j:j + 1, 0:CH] = bias[0:1] * hot[j]
     small[4:5, 0:CH] = head[0:1]
     extra = small[...]
-
-    x_out[0:CH] = sums_b[:, :TILE]
-    x_out[CH:2 * CH] = sums_b[:, TILE:]
     for e in range(BAND):
         s_out[e, 0:8] = gin_part[8 * e:8 * e + 8]
         s_out[e, 8:16] = extra
-    x_c, s_c = [], []
-    for e in (2, 3, 1):
-        dev = (r, band_at(e))
-        x_c.append(remote(x_out, x_in.at[e - 1], x_ss.at[e - 1], x_rs.at[e - 1], dev))
-        s_c.append(remote(s_out.at[band_at(e)], s_in.at[e - 1], s_ss.at[e - 1], s_rs.at[e - 1], dev))
-    for c, s in zip(x_c, s_c):
-        c.start()
-        s.start()
+    for c in s_c:
+        c.start()
     for c in e_c:
         c.wait_recv()
     for c, s in zip(x_c, s_c):
@@ -269,9 +296,9 @@
 
     g_c = [
         remote(
-            rs_out.at[lax.rem(g + d, GROUPS)], rs_in.at[d - 1], g_ss.at[d - 1], g_rs.at[d - 1], (group_at(d), b)
+            rs_out.at[group_index(dy, dx)], rs_in.at[n], g_ss.at[n], g_rs.at[n], (group_at(dy, dx), b)
         )
-        for d in (5, 3, 4, 6, 2, 7, 1)
+        for n, (dy, dx) in enumerate(GROUP_OFFSETS)
     ]
     for c in g_c:
         c.start()
@@ -289,7 +316,7 @@
         mine = mine + rs_in[d]
     zbuf[z] = mine.astype(BF16)
 
-    pl.semaphore_wait(here, 2)
+    pl.semaphore_wait(there, 2)
     z_c = [
         remote(
             zbuf.at[z], zbuf.at[z], z_ss.at[d - 1], z_rs.at[z], (ring_at(d), b)
@@ -317,15 +344,17 @@
     me = g * BAND + b
     fin[me] = whole.astype(BF16)
 
-    order = [(d, e) for d in range(GROUPS) for e in range(BAND) if d or e]
-    f_c = []
-    for n, (d, e) in enumerate(order):
-        f_c.append(remote(fin.at[me], fin.at[me], f_ss.at[n], f_rs.at[me], (group_at(d), band_at(e))))
+    f_c = [
+        remote(fin.at[me], fin.at[me], f_ss.at[n], f_rs.at[me], (group_at(dy, dx), band_at(dh, dc)))
+        for n, (dy, dx, dh, dc) in enumerate(ALL_OFFSETS)
+    ]
     for c in f_c:
         c.start()
-    for n, (d, e) in enumerate(order):
-        src = lax.rem(g + d, GROUPS) * BAND + band_at(e)
-        remote(fin.at[me], fin.at[src], f_ss.at[n], f_rs.at[src], (group_at(d), band_at(e))).wait_recv()
+    for n, (dy, dx, dh, dc) in reversed(list(enumerate(ALL_OFFSETS))):
+        src = group_index(dy, dx) * BAND + band_at(dh, dc)
+        remote(
+            fin.at[me], fin.at[src], f_ss.at[n], f_rs.at[src], (group_at(dy, dx), band_at(dh, dc))
+        ).wait_recv()
     for j in range(GROUPS):
         out = gl if j < 4 else gr
         for e in range(BAND):
@@ -353,6 +382,9 @@
 
 
 def on_device(emb, wl, wr, win, wout, whead, dbias, offsets, vbins, target):
+    def keep(x):
+        return pltpu.with_memory_space_constraint(x, pltpu.HBM)
+
     vm = pl.BlockSpec(memory_space=pltpu.VMEM)
     hbm = pl.BlockSpec(memory_space=pltpu.HBM)
     sd = jax.ShapeDtypeStruct
@@ -364,7 +396,7 @@
     outs = pl.pallas_call(
         kernel,
         out_shape=out_shape,
-        in_specs=[hbm] * 10,
+        in_specs=[hbm] * 7 + [pl.BlockSpec(memory_space=pltpu.SMEM)] + [hbm] * 2,
         out_specs=(vm,) * 8,
         scratch_shapes=[
             pltpu.VMEM((TILE, 512), BF16),
@@ -374,10 +406,9 @@
             pltpu.VMEM((CH, HID), BF16),
             pltpu.VMEM((1, CH), F32),
             pltpu.VMEM((NOFF, CH), F32),
-            pltpu.VMEM((1, 1), jnp.int32),
             pltpu.VMEM((1, TILE), jnp.int32),
             pltpu.VMEM((TILE, TILE), BF16),
-            dma((10,)),
+            dma((9,)),
             pltpu.VMEM((HID, TILE, TILE), F32),
             pltpu.VMEM((HID, TILE, TILE), F32),
             pltpu.VMEM((HID, TILE, TILE), F32),
@@ -402,15 +433,15 @@
             pltpu.VMEM((3, CH, TILE), BF16),
             dma((3,)), dma((3,)), dma((3,)), dma((3,)), dma((3,)), dma((3,)), dma((3,)), dma((3,)),
             dma((7,)), dma((7,)), dma((15,)), dma((16,)), dma((31,)), dma((32,)), dma((3,)), dma((3,)),
-            pltpu.SemaphoreType.REGULAR,
+            pltpu.SemaphoreType.REGULAR, pltpu.SemaphoreType.REGULAR,
         ],
         compiler_params=pltpu.CompilerParams(
             collective_id=0, has_side_effects=True, vmem_limit_bytes=48 * 1024 * 1024
         ),
         name="step",
     )(
-        emb, wl.T, wr.T, win, wout.T, whead.reshape(1, CH), dbias.T, offsets, vbins.reshape(1, TILE),
-        target.reshape(TILE, TILE),
+        keep(emb), keep(wl.T), keep(wr.T), keep(win), keep(wout.T), keep(whead.reshape(1, CH)), keep(dbias.T),
+        offsets, keep(vbins.reshape(1, TILE)), keep(target.reshape(TILE, TILE)),
     )
     pred, gemb, gl, gr, gin, gout, ghead, gbias = pl.pallas_call(
         write_out,

time: 58.5 us -> 50.2 us (0.86)
  local copies, waits for them, and re-layouts: 4.53 us -> 0 us
  Pallas kernels: 52.1 us -> 48.8 us
    unnamed x18 -> x0, local copies, waits for them, and re-layouts: 4.53 us -> none
    pallas_call x1, Pallas kernels: 51.4 us -> 48 us  [on_device(): pl.pallas_call(kernel, out_shape=out_shape, in_specs=[hbm] * 7 + [pl.Bloc...]
where the time goes in v3:
time: 50.2 us; the launch traced here: 50.1 us
  Pallas kernels  48.8 us (97%)
  between operations  1.29 us (3%)
    pallas_call x1, Pallas kernels, on_device(): pl.pallas_call(kernel, out_shape=out_shape, in_specs=[hbm] * 7 + [pl.Bloc...  48 us

profile of v3, /device:TPU:1, one launch (start us, length us, event | category | flops | bytes accessed | tf_op | source)
XLA Modules:
  0.0 50.1 jit_solution(4528623725067614612)
XLA Ops:
  1.3 48.0 %step.1 = (bf16[128,128]{1,0:T(8,128)(2,1)S(1)}, bf16[128,128]{1,0:T(8,128)(2,1)S(1)}, f32[32,512]{1,0:T(8,128)S(1)}, f32[32,512]{1,0:T(8,128)S(1)}, f32[32,128]...) custom-call(bf16[128,512]{1,0:T(8,128)(2,1)} %emb_h.1, ...), custom_call_target="tpu_custom_call" | custom-call | tf_op jit(solution)/shard_map/step/pallas_call | solution.py:396
  49.3 0.8 %write_out.1 = (bf16[128,128]{1,0:T(8,128)(2,1)}, bf16[128,128]{1,0:T(8,128)(2,1)}, f32[32,512]{1,0:T(8,128)}, f32[32,512]{1,0:T(8,128)}, f32[32,128]{1,0:T(8,12...) custom-call(bf16[128,128]{1,0:T(8,128)(2,1)S(1)} %get-tuple-element.24.refs_0_, ...), custom_call_target="tpu_custom_call" | custom-call | tf_op jit(solution)/shard_map/write_out/pallas_call | solution.py:446

commit v4 on v3

--- a/solution.py
+++ b/solution.py
@@ -55,10 +55,10 @@
     pred, gemb, gl, gr, gin, gout, ghead, gbias,
     emb, wl, wr, win, wout, whead, dbias, vbins, tgt, load_s,
     abc, act, slope, b_s, v_s, gr_s, gc_s, ar_s,
-    pay, pay_in, e_in,
+    pay, pay_in, flag_out, flag_in, off_out, off_in, e_in,
     x_out, x_in, s_out, s_in, small,
     rs_out, rs_in, zbuf, fin, c_out, c_in,
-    pay_ss, pay_rs, e_ss, e_rs, x_ss, x_rs, s_ss, s_rs, g_ss, g_rs, z_ss, z_rs, f_ss, f_rs, c_ss, c_rs, here, there,
+    pay_ss, pay_rs, flag_ss, flag_rs, off_ss, off_rs, e_ss, e_rs, x_ss, x_rs, s_ss, s_rs, g_ss, g_rs, z_ss, z_rs, f_ss, f_rs, c_ss, c_rs, here, there,
 ):
     r = lax.axis_index("rows")
     b = lax.axis_index("band")
@@ -117,14 +117,25 @@
     right_b = bdot(wr[...], emb[...], 1, 1).astype(BF16)
     right = right_b.astype(F32)
     flags = vbins[...].astype(F32)
-    pay[0:CH] = right_b
-    pay[CH:CH + 16] = jnp.broadcast_to(flags, (16, TILE)).astype(BF16)
+    pay[...] = right_b
+    flag_out[...] = jnp.broadcast_to(flags, (16, TILE)).astype(BF16)
 
     pl.semaphore_wait(barrier, len(near) + len(rest))
     pay_c = [
         remote(pay, pay_in.at[d - 1], pay_ss.at[d - 1], pay_rs.at[d - 1], (row_at(-d), b)) for d in (3, 2, 1)
     ]
     for c in pay_c:
+        c.start()
+    flag_c = [
+        remote(flag_out, flag_in.at[d - 1], flag_ss.at[d - 1], flag_rs.at[d - 1], (row_at(-d), b)) for d in (3, 2, 1)
+    ]
+    offset = off_h[0, 0]
+    off_out[...] = jnp.full((8, TILE), offset.astype(F32), F32)
+    off_c = [
+        remote(off_out, off_in.at[n], off_ss.at[n], off_rs.at[n], (r, band_at(dh, dc)))
+        for n, (dh, dc) in enumerate(BAND_OFFSETS)
+    ]
+    for c in flag_c + off_c:
         c.start()
     for dy, dx in GROUP_OFFSETS:
         signal(here, (group_at(dy, dx), b))
@@ -148,7 +159,6 @@
     wcol_lin = wcol + 0.5 * jnp.sum(win_f * v_row, axis=1, keepdims=True)
     wrow_lin = jnp.sum(jnp.where(eye, wcol_lin, 0.0), axis=0, keepdims=True)
     row_logit = jnp.sum(ltf * wrow_lin, axis=1, keepdims=True)
-    offset = off_h[0, 0]
     hot = [jnp.where(offset == j, 1.0, 0.0).astype(F32) for j in range(NOFF)]
     bias_row = sum(dbias[j:j + 1, :] * hot[j] for j in range(NOFF))
     bias_col = jnp.sum(jnp.where(eye, bias_row, 0.0), axis=1, keepdims=True)
@@ -169,19 +179,19 @@
         return pltpu.roll(rolled, TILE - 8, 1)
 
     lax.fori_loop(0, HID // 8, spread, at)
+    for j in range(GROUPS):
+        rs_out[j, 8:16] = jnp.zeros((8, TILE), F32)
 
     pl.semaphore_wait(here, len(GROUP_OFFSETS) + 2)
     for d in (4, 12):
         signal(there, (ring_at(d), b))
 
-    r_sel = right * hot[0]
-    f_sel = flags * hot[0]
+    weight = [hot[0]] + [hot[d] * jnp.where(r + d < ROWS, 1.0, 0.0).astype(F32) for d in (1, 2, 3)]
+    r_sel = right * weight[0]
     for c in pay_c:
         c.wait_recv()
     for d in (1, 2, 3):
-        keep = hot[d] * jnp.where(r + d < ROWS, 1.0, 0.0).astype(F32)
-        r_sel = r_sel + pay_in[d - 1, 0:CH].astype(F32) * keep
-        f_sel = f_sel + pay_in[d - 1, CH:CH + 16].astype(F32)[0:1] * keep
+        r_sel = r_sel + pay_in[d - 1].astype(F32) * weight[d]
 
     e_c = [
         remote(emb.at[:, share], e_in.at[d - 1], e_ss.at[d - 1], e_rs.at[d - 1], (row_at(-d), b)) for d in (3, 2, 1)
@@ -208,23 +218,23 @@
     total = lax.fori_loop(0, HID // 8, first, jnp.zeros((TILE, TILE), F32))
     logits = total * (0.5 * ALPHA) + (row_logit + col_logit)
     pred[...] = logits.astype(BF16)
+    f_sel = flags * weight[0]
+    for c in flag_c:
+        c.wait_recv()
+    for d in (1, 2, 3):
+        f_sel = f_sel + flag_in[d - 1, 0:1].astype(F32) * weight[d]
     res = (row_flags * f_sel) * (logits - tgt_f) * (1.0 / (NOFF * TILE))
     ones = jnp.ones((8, TILE), BF16)
 
-    def second(i, carry):
-        parts = []
-        for j in range(32):
-            k = 32 * i + j
-            h = slope[k] * res
-            gc_s[pl.ds(k, 1), :] = jnp.sum(h, axis=0, keepdims=True)
-            ar_s[pl.ds(k, 1), :] = jnp.sum(act[k] * res, axis=0, keepdims=True)
-            parts.append(h.astype(BF16))
-        over_q = bdot(ones, jnp.concatenate(parts, axis=0), 1, 1)
-        for j in range(32):
-            gr_s[pl.ds(32 * i + j, 1), :] = over_q[0:1, TILE * j:TILE * (j + 1)]
-        return carry
-
-    lax.fori_loop(0, HID // 32, second, 0)
+    parts = []
+    for k in range(HID):
+        h = slope[k] * res
+        gc_s[k:k + 1, :] = jnp.sum(h, axis=0, keepdims=True)
+        ar_s[k:k + 1, :] = jnp.sum(act[k] * res, axis=0, keepdims=True)
+        parts.append(h.astype(BF16))
+    over_q = bdot(ones, jnp.concatenate(parts, axis=0), 1, 1)
+    for k in range(HID):
+        gr_s[k:k + 1, :] = over_q[0:1, TILE * k:TILE * (k + 1)]
 
     half_v = v_s[...] * 0.5
     res_hi, res_lo = halves(res)
@@ -254,7 +264,7 @@
     bias = hdot(ones_f, sums[:, :TILE], 1, 1)
     ar = hdot(ones_f, ar_s[...], 1, 1) + hdot(head, win_f, 1, 0) * (1.0 / ALPHA)
     row_id = lax.broadcasted_iota(jnp.int32, (8, TILE), 0)
-    small[...] = jnp.where(row_id == 5, ar, jnp.where(row_id == 6, offset.astype(F32), 0.0))
+    small[...] = jnp.where(row_id == 5, ar, 0.0)
     for j in range(NOFF):
         small[j:j + 1, 0:CH] = bias[0:1] * hot[j]
     small[4:5, 0:CH] = head[0:1]
@@ -264,23 +274,17 @@
         s_out[e, 8:16] = extra
     for c in s_c:
         c.start()
-    for c in e_c:
-        c.wait_recv()
-    for c, s in zip(x_c, s_c):
-        c.wait_recv()
-        s.wait_recv()
-    own = x_out[...].astype(F32)
-    row_tot = own[:CH]
-    cols = [own[CH:] * hot[j] for j in range(NOFF)]
-    mine = s_out[b]
-    for e in range(BAND - 1):
-        got = x_in[e].astype(F32)
-        its = s_in[e]
+    for c in e_c + off_c + x_c:
+        c.wait_recv()
+    own = sums_b.astype(F32)
+    row_tot = own[:, :TILE]
+    cols = [own[:, TILE:] * hot[j] for j in range(NOFF)]
+    for n in range(BAND - 1):
+        got = x_in[n].astype(F32)
         row_tot = row_tot + got[:CH]
-        its_offset = its[14:15, :]
+        its_offset = off_in[n, 0:1, :]
         for j in range(NOFF):
             cols[j] = cols[j] + jnp.where(its_offset == j, got[CH:], 0.0)
-        mine = mine + its
     row_b = row_tot.astype(BF16)
     cols_b = [c.astype(BF16) for c in cols]
     part_l = bdot(row_b, emb[:, share], 1, 0)
@@ -290,9 +294,14 @@
     for j in range(4):
         rs_out[j, 0:8] = part_l[8 * j:8 * j + 8]
         rs_out[4 + j, 0:8] = part_r[8 * j:8 * j + 8]
-    zero = jnp.zeros((6, TILE), F32)
+    mine = s_out[b]
+    for c in s_c:
+        c.wait_recv()
+    for n in range(BAND - 1):
+        mine = mine + s_in[n]
     for j in range(GROUPS):
-        rs_out[j, 8:16] = jnp.concatenate([mine[j:j + 1], mine[8 + j:9 + j], zero], axis=0)
+        rs_out[j, 8:9] = mine[j:j + 1]
+        rs_out[j, 9:10] = mine[8 + j:9 + j]
 
     g_c = [
         remote(
@@ -368,7 +377,7 @@
     ghead[...] = small[4:5, 0:CH] + hdot(jnp.broadcast_to(ar_row, (8, TILE)), wout_f, 1, 1)[0:1]
     gbias[...] = small[0:NOFF, 0:CH]
 
-    for c in pay_c + e_c + x_c + s_c + g_c + c_c + z_c + f_c:
+    for c in pay_c + flag_c + off_c + e_c + x_c + s_c + g_c + c_c + z_c + f_c:
         c.wait_send()
 
 
@@ -417,8 +426,12 @@
             pltpu.VMEM((HID, TILE), F32),
             pltpu.VMEM((HID, TILE), F32),
             pltpu.VMEM((HID, TILE), F32),
-            pltpu.VMEM((48, TILE), BF16),
-            pltpu.VMEM((3, 48, TILE), BF16),
+            pltpu.VMEM((CH, TILE), BF16),
+            pltpu.VMEM((3, CH, TILE), BF16),
+            pltpu.VMEM((16, TILE), BF16),
+            pltpu.VMEM((3, 16, TILE), BF16),
+            pltpu.VMEM((8, TILE), F32),
+            pltpu.VMEM((3, 8, TILE), F32),
             pltpu.VMEM((3, TILE, TILE), BF16),
             pltpu.VMEM((2 * CH, TILE), BF16),
             pltpu.VMEM((3, 2 * CH, TILE), BF16),
@@ -431,8 +444,8 @@
             pltpu.VMEM((GROUPS * BAND, 16, TILE), BF16),
             pltpu.VMEM((3, CH, TILE), BF16),
             pltpu.VMEM((3, CH, TILE), BF16),
-            dma((3,)), dma((3,)), dma((3,)), dma((3,)), dma((3,)), dma((3,)), dma((3,)), dma((3,)),
-            dma((7,)), dma((7,)), dma((15,)), dma((16,)), dma((31,)), dma((32,)), dma((3,)), dma((3,)),
+            dma((3,)), dma((3,)), dma((3,)), dma((3,)), dma((3,)), dma((3,)), dma((3,)), dma((3,)), dma((3,)), dma((3,)),
+            dma((3,)), dma((3,)), dma((7,)), dma((7,)), dma((15,)), dma((16,)), dma((31,)), dma((32,)), dma((3,)), dma((3,)),
             pltpu.SemaphoreType.REGULAR, pltpu.SemaphoreType.REGULAR,
         ],
         compiler_params=pltpu.CompilerParams(

time: 50.2 us -> 49.5 us (0.986)
  Pallas kernels: 48.8 us -> 48 us
    pallas_call x1, Pallas kernels: 48 us -> 47.3 us  [on_device(): pl.pallas_call(kernel, out_shape=out_shape, in_specs=[hbm] * 7 + [pl.Bloc...]
where the time goes in v4:
time: 49.5 us; the launch traced here: 49.3 us
  Pallas kernels  48 us (97%)
  between operations  1.29 us (3%)
    pallas_call x1, Pallas kernels, on_device(): pl.pallas_call(kernel, out_shape=out_shape, in_specs=[hbm] * 7 + [pl.Bloc...  47.3 us

profile of v4, /device:TPU:1, one launch (start us, length us, event | category | flops | bytes accessed | tf_op | source)
XLA Modules:
  0.0 49.3 jit_solution(15891704456436169797)
XLA Ops:
  1.3 47.3 %step.1 = (bf16[128,128]{1,0:T(8,128)(2,1)S(1)}, bf16[128,128]{1,0:T(8,128)(2,1)S(1)}, f32[32,512]{1,0:T(8,128)S(1)}, f32[32,512]{1,0:T(8,128)S(1)}, f32[32,128]...) custom-call(bf16[128,512]{1,0:T(8,128)(2,1)} %emb_h.1, ...), custom_call_target="tpu_custom_call" | custom-call | tf_op jit(solution)/shard_map/step/pallas_call | solution.py:405
  48.6 0.8 %write_out.1 = (bf16[128,128]{1,0:T(8,128)(2,1)}, bf16[128,128]{1,0:T(8,128)(2,1)}, f32[32,512]{1,0:T(8,128)}, f32[32,512]{1,0:T(8,128)}, f32[32,128]{1,0:T(8,12...) custom-call(bf16[128,128]{1,0:T(8,128)(2,1)S(1)} %get-tuple-element.24.refs_0_, ...), custom_call_target="tpu_custom_call" | custom-call | tf_op jit(solution)/shard_map/write_out/pallas_call | solution.py:459

commit v5 on v4

--- a/solution.py
+++ b/solution.py
@@ -54,7 +54,7 @@
     emb_h, wl_h, wr_h, win_h, wout_h, whead_h, dbias_h, off_h, vbins_h, tgt_h,
     pred, gemb, gl, gr, gin, gout, ghead, gbias,
     emb, wl, wr, win, wout, whead, dbias, vbins, tgt, load_s,
-    abc, act, slope, b_s, v_s, gr_s, gc_s, ar_s,
+    lhs, spread, act, slope, b_s, v_s, gr_s, gc_s, ar_s,
     pay, pay_in, flag_out, flag_in, off_out, off_in, e_in,
     x_out, x_in, s_out, s_in, small,
     rs_out, rs_in, zbuf, fin, c_out, c_in,
@@ -145,7 +145,6 @@
     share = pl.ds(pl.multiple_of(b * TILE, TILE), TILE)
     left = bdot(wl[...], emb[...], 1, 1).astype(BF16).astype(F32)
     ltf = jnp.transpose(left)
-    lt = ltf.astype(BF16)
     for c in loads[4:]:
         c.wait()
     wh = whead[...]
@@ -171,14 +170,22 @@
         axis=1, keepdims=True,
     )
     tgt_f = tgt[...].astype(F32)
-    at = bdot(lt, win[...], 1, 0) * (1.0 / ALPHA)
-
-    def spread(i, rolled):
-        for j in range(8):
-            abc[8 * i + j] = jnp.broadcast_to(rolled[:, j:j + 1], (TILE, TILE))
-        return pltpu.roll(rolled, TILE - 8, 1)
-
-    lax.fori_loop(0, HID // 8, spread, at)
+    a = bdot(win_t.astype(BF16), left.astype(BF16), 1, 0) * (1.0 / ALPHA)
+    a_hi = a.astype(BF16).astype(F32)
+    a_lo = a - a_hi
+    ones_16 = jnp.ones((16, TILE), F32)
+    for m in range(4):
+        parts = []
+        for i in range(4 * m, 4 * m + 4):
+            parts += [a_hi[8 * i:8 * i + 8], a_lo[8 * i:8 * i + 8], ones_16]
+        turned = jnp.transpose(jnp.concatenate(parts, axis=0)).astype(BF16)
+        for i in range(4):
+            lhs[4 * m + i] = turned[:, 32 * i:32 * i + 32]
+    spread[...] = jnp.where(
+        lax.rem(lax.broadcasted_iota(jnp.int32, (16, 8 * TILE), 0), 8)
+        == lax.div(lax.broadcasted_iota(jnp.int32, (16, 8 * TILE), 1), TILE),
+        1.0, 0.0,
+    ).astype(BF16)
     for j in range(GROUPS):
         rs_out[j, 8:16] = jnp.zeros((8, TILE), F32)
 
@@ -202,11 +209,19 @@
     r_b = r_sel + bias_col
     b_s[...] += bdot(win_t.astype(BF16), r_sel.astype(BF16), 1, 0) * (1.0 / ALPHA)
     col_logit = jnp.sum(r_b * wcol_lin, axis=0, keepdims=True)
+    p_hi, p_lo = halves(jnp.concatenate([left, r_b], axis=1))
+    p_3 = jnp.concatenate([p_hi, p_hi, p_lo], axis=1)
 
     def first(i, total):
+        b8 = b_s[pl.ds(pl.multiple_of(8 * i, 8), 8), :]
+        b_hi = b8.astype(BF16).astype(F32)
+        b_16 = jnp.concatenate([b_hi, b8 - b_hi], axis=0).astype(BF16)
+        mask = spread[...]
+        rhs = jnp.concatenate([mask, jnp.concatenate([b_16] * 8, axis=1) * mask], axis=0)
+        y_8 = bdot(lhs[i], rhs, 1, 0)
         for j in range(8):
             k = 8 * i + j
-            y = abc[k] + b_s[pl.ds(k, 1), :]
+            y = y_8[:, TILE * j:TILE * (j + 1)]
             w = y * y + BETA
             t = jnp.tanh(y * w)
             yt = y * t
@@ -215,7 +230,7 @@
             total = total + yt * v_s[pl.ds(k, 1), :]
         return total
 
-    total = lax.fori_loop(0, HID // 8, first, jnp.zeros((TILE, TILE), F32))
+    total = lax.fori_loop(0, HID // 8, first, jnp.zeros((TILE, TILE), F32), unroll=4)
     logits = total * (0.5 * ALPHA) + (row_logit + col_logit)
     pred[...] = logits.astype(BF16)
     f_sel = flags * weight[0]
@@ -257,12 +272,15 @@
         s_c.append(remote(s_out.at[band_at(dh, dc)], s_in.at[n], s_ss.at[n], s_rs.at[n], dev))
     for c in x_c:
         c.start()
-    p_both = jnp.concatenate([left, r_b], axis=1)
-    gin_part = hdot(p_both, g_both, 1, 1)
-    head = hdot(r_both, p_both, 1, 1)
-    ones_f = jnp.ones((8, TILE), F32)
-    bias = hdot(ones_f, sums[:, :TILE], 1, 1)
-    ar = hdot(ones_f, ar_s[...], 1, 1) + hdot(head, win_f, 1, 0) * (1.0 / ALPHA)
+    r_hi, r_lo = halves(r_both)
+    gin_part = bdot(p_3, jnp.concatenate([g_hi, g_lo, g_hi], axis=1), 1, 1)
+    head = bdot(jnp.concatenate([r_hi, r_lo, r_hi], axis=1), p_3, 1, 1)
+    ones_2 = jnp.ones((8, 2 * TILE), BF16)
+    bias = bdot(ones_2, jnp.concatenate(halves(sums[:, :TILE]), axis=1), 1, 1)
+    h_hi, h_lo = halves(head)
+    ar = bdot(ones_2, jnp.concatenate(halves(ar_s[...]), axis=1), 1, 1) + bdot(
+        jnp.concatenate([h_hi, h_lo], axis=1), jnp.concatenate([win[...], win[...]], axis=0), 1, 0
+    ) * (1.0 / ALPHA)
     row_id = lax.broadcasted_iota(jnp.int32, (8, TILE), 0)
     small[...] = jnp.where(row_id == 5, ar, 0.0)
     for j in range(NOFF):
@@ -287,10 +305,11 @@
             cols[j] = cols[j] + jnp.where(its_offset == j, got[CH:], 0.0)
     row_b = row_tot.astype(BF16)
     cols_b = [c.astype(BF16) for c in cols]
-    part_l = bdot(row_b, emb[:, share], 1, 0)
-    part_r = bdot(cols_b[0], emb[:, share], 1, 0)
-    for d in (1, 2, 3):
-        part_r = part_r + bdot(cols_b[d], e_in[d - 1], 1, 0)
+    near_part = bdot(jnp.concatenate([row_b, cols_b[0]], axis=0), emb[:, share], 1, 0)
+    part_l = near_part[:CH]
+    part_r = near_part[CH:] + bdot(
+        jnp.concatenate(cols_b[1:], axis=1), jnp.concatenate([e_in[d] for d in range(3)], axis=0), 1, 0
+    )
     for j in range(4):
         rs_out[j, 0:8] = part_l[8 * j:8 * j + 8]
         rs_out[4 + j, 0:8] = part_r[8 * j:8 * j + 8]
@@ -374,7 +393,10 @@
                 small[j:j + 1, :] = chunk[9:10]
     ar_row = small[5:6, :] * (0.5 * ALPHA)
     gout[...] = wcol * ar_row
-    ghead[...] = small[4:5, 0:CH] + hdot(jnp.broadcast_to(ar_row, (8, TILE)), wout_f, 1, 1)[0:1]
+    ghead[...] = small[4:5, 0:CH] + bdot(
+        jnp.concatenate(halves(jnp.broadcast_to(ar_row, (8, TILE))), axis=1),
+        jnp.concatenate([wout[...], wout[...]], axis=1), 1, 1,
+    )[0:1]
     gbias[...] = small[0:NOFF, 0:CH]
 
     for c in pay_c + flag_c + off_c + e_c + x_c + s_c + g_c + c_c + z_c + f_c:
@@ -418,7 +440,8 @@
             pltpu.VMEM((1, TILE), jnp.int32),
             pltpu.VMEM((TILE, TILE), BF16),
             dma((9,)),
-            pltpu.VMEM((HID, TILE, TILE), F32),
+            pltpu.VMEM((HID // 8, TILE, 32), BF16),
+            pltpu.VMEM((16, 8 * TILE), BF16),
             pltpu.VMEM((HID, TILE, TILE), F32),
             pltpu.VMEM((HID, TILE, TILE), F32),
             pltpu.VMEM((HID, TILE), F32),

time: 49.5 us -> 49.2 us (level)
  no operation moved by 1% of the time
where the time goes in v5:
time: 49.2 us; the launch traced here: 49 us
  Pallas kernels  47.7 us (97%)
  between operations  1.29 us (3%)
    pallas_call x1, Pallas kernels, on_device(): pl.pallas_call(kernel, out_shape=out_shape, in_specs=[hbm] * 7 + [pl.Bloc...  47 us

profile of v5, /device:TPU:1, one launch (start us, length us, event | category | flops | bytes accessed | tf_op | source)
XLA Modules:
  0.0 49.0 jit_solution(14084997810407446340)
XLA Ops:
  1.3 47.0 %step.1 = (bf16[128,128]{1,0:T(8,128)(2,1)S(1)}, bf16[128,128]{1,0:T(8,128)(2,1)S(1)}, f32[32,512]{1,0:T(8,128)S(1)}, f32[32,512]{1,0:T(8,128)S(1)}, f32[32,128]...) custom-call(bf16[128,512]{1,0:T(8,128)(2,1)} %emb_h.1, ...), custom_call_target="tpu_custom_call" | custom-call | tf_op jit(solution)/shard_map/step/pallas_call | solution.py:427
  48.3 0.8 %write_out.1 = (bf16[128,128]{1,0:T(8,128)(2,1)}, bf16[128,128]{1,0:T(8,128)(2,1)}, f32[32,512]{1,0:T(8,128)}, f32[32,512]{1,0:T(8,128)}, f32[32,128]{1,0:T(8,12...) custom-call(bf16[128,128]{1,0:T(8,128)(2,1)S(1)} %get-tuple-element.24.refs_0_, ...), custom_call_target="tpu_custom_call" | custom-call | tf_op jit(solution)/shard_map/write_out/pallas_call | solution.py:482

commit v6 on v5

--- a/solution.py
+++ b/solution.py
@@ -56,7 +56,7 @@
     emb, wl, wr, win, wout, whead, dbias, vbins, tgt, load_s,
     lhs, spread, act, slope, b_s, v_s, gr_s, gc_s, ar_s,
     pay, pay_in, flag_out, flag_in, off_out, off_in, e_in,
-    x_out, x_in, s_out, s_in, small,
+    x_out, x_in, s_out, s_in, small, tail,
     rs_out, rs_in, zbuf, fin, c_out, c_in,
     pay_ss, pay_rs, flag_ss, flag_rs, off_ss, off_rs, e_ss, e_rs, x_ss, x_rs, s_ss, s_rs, g_ss, g_rs, z_ss, z_rs, f_ss, f_rs, c_ss, c_rs, here, there,
 ):
@@ -186,8 +186,7 @@
         == lax.div(lax.broadcasted_iota(jnp.int32, (16, 8 * TILE), 1), TILE),
         1.0, 0.0,
     ).astype(BF16)
-    for j in range(GROUPS):
-        rs_out[j, 8:16] = jnp.zeros((8, TILE), F32)
+    tail[...] = jnp.zeros_like(tail)
 
     pl.semaphore_wait(here, len(GROUP_OFFSETS) + 2)
     for d in (4, 12):
@@ -237,7 +236,7 @@
     for c in flag_c:
         c.wait_recv()
     for d in (1, 2, 3):
-        f_sel = f_sel + flag_in[d - 1, 0:1].astype(F32) * weight[d]
+        f_sel = f_sel + flag_in[d - 1].astype(F32)[0:1] * weight[d]
     res = (row_flags * f_sel) * (logits - tgt_f) * (1.0 / (NOFF * TILE))
     ones = jnp.ones((8, TILE), BF16)
 
@@ -310,17 +309,18 @@
     part_r = near_part[CH:] + bdot(
         jnp.concatenate(cols_b[1:], axis=1), jnp.concatenate([e_in[d] for d in range(3)], axis=0), 1, 0
     )
-    for j in range(4):
-        rs_out[j, 0:8] = part_l[8 * j:8 * j + 8]
-        rs_out[4 + j, 0:8] = part_r[8 * j:8 * j + 8]
     mine = s_out[b]
     for c in s_c:
         c.wait_recv()
     for n in range(BAND - 1):
         mine = mine + s_in[n]
     for j in range(GROUPS):
-        rs_out[j, 8:9] = mine[j:j + 1]
-        rs_out[j, 9:10] = mine[8 + j:9 + j]
+        tail[j, 0:1] = mine[j:j + 1]
+        tail[j, 1:2] = mine[8 + j:9 + j]
+    for j in range(GROUPS):
+        part = part_l if j < 4 else part_r
+        at_j = 8 * (j % 4)
+        rs_out[j] = jnp.concatenate([part[at_j:at_j + 8], tail[j]], axis=0).astype(BF16)
 
     g_c = [
         remote(
@@ -337,11 +337,11 @@
     ]
     for c in c_c:
         c.start()
-    mine = rs_out[g]
+    mine = rs_out[g].astype(F32)
     for c in g_c:
         c.wait_recv()
     for d in range(GROUPS - 1):
-        mine = mine + rs_in[d]
+        mine = mine + rs_in[d].astype(F32)
     zbuf[z] = mine.astype(BF16)
 
     pl.semaphore_wait(there, 2)
@@ -461,8 +461,9 @@
             pltpu.VMEM((BAND, 16, TILE), F32),
             pltpu.VMEM((3, 16, TILE), F32),
             pltpu.VMEM((8, TILE), F32),
-            pltpu.VMEM((GROUPS, 16, TILE), F32),
-            pltpu.VMEM((GROUPS - 1, 16, TILE), F32),
+            pltpu.VMEM((GROUPS, 8, TILE), F32),
+            pltpu.VMEM((GROUPS, 16, TILE), BF16),
+            pltpu.VMEM((GROUPS - 1, 16, TILE), BF16),
             pltpu.VMEM((RING, 16, TILE), BF16),
             pltpu.VMEM((GROUPS * BAND, 16, TILE), BF16),
             pltpu.VMEM((3, CH, TILE), BF16),

time: 49.2 us -> 49 us (level)
  no operation moved by 1% of the time
where the time goes in v6:
time: 49 us; the launch traced here: 48.9 us
  Pallas kernels  47.6 us (97%)
  between operations  1.29 us (3%)
    pallas_call x1, Pallas kernels, on_device(): pl.pallas_call(kernel, out_shape=out_shape, in_specs=[hbm] * 7 + [pl.Bloc...  46.9 us

profile of v6, /device:TPU:1, one launch (start us, length us, event | category | flops | bytes accessed | tf_op | source)
XLA Modules:
  0.0 48.9 jit_solution(12352943760077120871)
XLA Ops:
  1.3 46.9 %step.1 = (bf16[128,128]{1,0:T(8,128)(2,1)S(1)}, bf16[128,128]{1,0:T(8,128)(2,1)S(1)}, f32[32,512]{1,0:T(8,128)S(1)}, f32[32,512]{1,0:T(8,128)S(1)}, f32[32,128]...) custom-call(bf16[128,512]{1,0:T(8,128)(2,1)} %emb_h.1, ...), custom_call_target="tpu_custom_call" | custom-call | tf_op jit(solution)/shard_map/step/pallas_call | solution.py:427
  48.1 0.8 %write_out.1 = (bf16[128,128]{1,0:T(8,128)(2,1)}, bf16[128,128]{1,0:T(8,128)(2,1)}, f32[32,512]{1,0:T(8,128)}, f32[32,512]{1,0:T(8,128)}, f32[32,128]{1,0:T(8,12...) custom-call(bf16[128,128]{1,0:T(8,128)(2,1)S(1)} %get-tuple-element.24.refs_0_, ...), custom_call_target="tpu_custom_call" | custom-call | tf_op jit(solution)/shard_map/write_out/pallas_call | solution.py:483

commit v7 on v6

--- a/solution.py
+++ b/solution.py
@@ -240,6 +240,11 @@
     res = (row_flags * f_sel) * (logits - tgt_f) * (1.0 / (NOFF * TILE))
     ones = jnp.ones((8, TILE), BF16)
 
+    res_hi, res_lo = halves(res)
+    rr = bdot(jnp.ones((8, 2 * TILE), BF16), jnp.concatenate([res_hi, res_lo], axis=1), 1, 1)
+    rc = jnp.broadcast_to(jnp.sum(res, axis=0, keepdims=True), (8, TILE))
+    r_both = jnp.concatenate([rr, rc], axis=1)
+    half_v = v_s[...] * 0.5
     parts = []
     for k in range(HID):
         h = slope[k] * res
@@ -250,11 +255,6 @@
     for k in range(HID):
         gr_s[k:k + 1, :] = over_q[0:1, TILE * k:TILE * (k + 1)]
 
-    half_v = v_s[...] * 0.5
-    res_hi, res_lo = halves(res)
-    rr = bdot(jnp.ones((8, 2 * TILE), BF16), jnp.concatenate([res_hi, res_lo], axis=1), 1, 1)
-    rc = jnp.broadcast_to(jnp.sum(res, axis=0, keepdims=True), (8, TILE))
-    r_both = jnp.concatenate([rr, rc], axis=1)
     g_both = jnp.concatenate([(gr_s[...] + rr[0:1]) * half_v, (gc_s[...] + rc[0:1]) * half_v], axis=1)
     g_hi, g_lo = halves(g_both)
     sums = wcol * r_both[0:1] + bdot(

time: 49 us -> 49 us (level)
  no operation moved by 1% of the time
where the time goes in v7:
time: 49 us; the launch traced here: 48.9 us
  Pallas kernels  47.6 us (97%)
  between operations  1.29 us (3%)
    pallas_call x1, Pallas kernels, on_device(): pl.pallas_call(kernel, out_shape=out_shape, in_specs=[hbm] * 7 + [pl.Bloc...  46.8 us

profile of v7, /device:TPU:1, one launch (start us, length us, event | category | flops | bytes accessed | tf_op | source)
XLA Modules:
  0.0 48.9 jit_solution(8676637074897284906)
XLA Ops:
  1.3 46.8 %step.1 = (bf16[128,128]{1,0:T(8,128)(2,1)S(1)}, bf16[128,128]{1,0:T(8,128)(2,1)S(1)}, f32[32,512]{1,0:T(8,128)S(1)}, f32[32,512]{1,0:T(8,128)S(1)}, f32[32,128]...) custom-call(bf16[128,512]{1,0:T(8,128)(2,1)} %emb_h.1, ...), custom_call_target="tpu_custom_call" | custom-call | tf_op jit(solution)/shard_map/step/pallas_call | solution.py:427
  48.1 0.8 %write_out.1 = (bf16[128,128]{1,0:T(8,128)(2,1)}, bf16[128,128]{1,0:T(8,128)(2,1)}, f32[32,512]{1,0:T(8,128)}, f32[32,512]{1,0:T(8,128)}, f32[32,128]{1,0:T(8,12...) custom-call(bf16[128,128]{1,0:T(8,128)(2,1)S(1)} %get-tuple-element.24.refs_0_, ...), custom_call_target="tpu_custom_call" | custom-call | tf_op jit(solution)/shard_map/write_out/pallas_call | solution.py:483
